TPU v7x, 256 devices: a whole 4x4x8 slice. The times are simulated.
256 devices in a mesh: dom: 32 (over x_hi, z, core), ka: 8 (over x_lo, y).
Axes of the slice: x: 4 (x_hi: 2, x_lo: 2; x = x_hi * 2 + x_lo), y: 4, z: 8, core: 2. Of those that a mesh axis runs over, the one named last changes fastest.
Arguments:
- frac: float32 [3, 131072], P(None, 'dom'), may hold values from 0 to 1
- species: int32 [131072], P('dom'), may hold values from 0 to 7
- feats: bfloat16 [131072, 256], P('dom'), may hold values from -6 to 6
- cotangent: bfloat16 [131072, 256], P('dom'), may hold values from -6 to 6
- miller: int32 [3, 2048], P(None, 'ka'), may hold values from -8 to 8, as said below
- species_gain: float32 [8, 256], replicated, may hold values from 0.1 to 1.9
- filter_weight: float32 [16, 256], replicated, may hold values from -4 to 4
Outputs:
- updated: bfloat16 [131072, 256], P('dom')
- forces: float32 [3, 131072], P(None, 'dom')
Inputs may be any that keep to these rules, and one draw needn't show every extreme that they name: `miller`: no k-vector has all three indices zero; both -8 and 8 occur.
All inputs are finite; a program needn't handle non-finite values.
Results may differ from a plain program's by a relative error of at most 0.006.
Values may be sent and summed in bfloat16 or wider, within the bound.
No kernel may reach another device: no remote copies, remote signals or barrier semaphores. Data moves between devices by JAX's collectives and lax.ppermute only.
A program may use at most 64 MiB of HBM per device.

v0:
```python
import math

import jax
import jax.numpy as jnp
from jax import lax
from jax.sharding import PartitionSpec as P

TWO_PI = 6.283185307179586
BOX = 64.0


def phase_tables(frac, miller):
    theta = TWO_PI * lax.dot_general(
        frac, miller.astype(jnp.float32), (((0,), (0,)), ((), ())), precision=lax.Precision.HIGHEST
    )
    return (jnp.cos(theta).astype(jnp.bfloat16), jnp.sin(theta).astype(jnp.bfloat16))


def kernel_weights(miller, filter_weight):
    mills = miller.astype(jnp.float32)
    length = jnp.sqrt(jnp.sum(mills * mills, axis=0))
    count = filter_weight.shape[0]
    centres = jnp.arange(count, dtype=jnp.float32) * (14.0 / (count - 1))
    basis = jnp.exp(-((length[:, None] - centres[None, :]) ** 2))
    return jnp.dot(basis, filter_weight, precision=lax.Precision.HIGHEST)


def species_rows(feats, species, species_gain):
    onehot = (
        species[:, None] == jnp.arange(species_gain.shape[0], dtype=jnp.int32)[None, :]
    ).astype(jnp.float32)
    gains = jnp.dot(onehot, species_gain, precision=lax.Precision.HIGHEST)
    return (feats.astype(jnp.float32) * gains).astype(jnp.bfloat16)


def project(table, rows):
    return lax.dot_general(
        table, rows, (((0,), (0,)), ((), ())), preferred_element_type=jnp.float32
    )


def against(left, panel):
    return lax.dot_general(
        left, panel, (((1,), (1,)), ((), ())), preferred_element_type=jnp.float32
    )


def angle_grad(cos_t, sin_t, cotangent, embedded, panels, inv_k, inv_n):
    fr, fi, ar, ai = panels
    cosf = cos_t.astype(jnp.float32)
    sinf = sin_t.astype(jnp.float32)
    direct = -sinf * against(cotangent, fr) + cosf * against(cotangent, fi)
    through = -sinf * against(embedded, ar) + cosf * against(embedded, ai)
    return direct * inv_k + through * inv_n


def force_terms(miller, grads):
    return (
        -TWO_PI
        / BOX
        * lax.dot_general(
            miller.astype(jnp.float32),
            grads,
            (((1,), (1,)), ((), ())),
            precision=lax.Precision.HIGHEST,
        )
    )


def body(frac, species, feats, cotangent, miller, species_gain, filter_weight):
    inv_n = 1.0 / math.sqrt(feats.shape[0] * lax.axis_size("dom"))
    inv_k = 1.0 / math.sqrt(miller.shape[1] * lax.axis_size("ka"))
    cos_t, sin_t = phase_tables(frac, miller)
    weights = kernel_weights(miller, filter_weight)
    embedded = species_rows(feats, species, species_gain)
    terms = (
        project(cos_t, embedded),
        project(sin_t, embedded),
        project(cos_t, cotangent),
        project(sin_t, cotangent),
    )
    sr, si, gr, gi = lax.psum((terms[0], terms[1], terms[2], terms[3]), "dom")
    fr = (weights * sr * inv_n).astype(jnp.bfloat16)
    fi = (weights * si * inv_n).astype(jnp.bfloat16)
    ar = (weights * gr * inv_k).astype(jnp.bfloat16)
    ai = (weights * gi * inv_k).astype(jnp.bfloat16)
    message_part = jnp.dot(cos_t, fr, preferred_element_type=jnp.float32) + jnp.dot(
        sin_t, fi, preferred_element_type=jnp.float32
    )
    grads = angle_grad(cos_t, sin_t, cotangent, embedded, (fr, fi, ar, ai), inv_k, inv_n)
    force_part = force_terms(miller, grads)
    total, forces = lax.psum((message_part, force_part), "ka")
    updated = (feats.astype(jnp.float32) + total * inv_k).astype(jnp.bfloat16)
    return (updated, forces)


def solution(mesh):
    placed = (P(None, "dom"), P("dom"), P("dom", None), P("dom", None), P(None, "ka"), P(), P())
    return jax.shard_map(
        body,
        mesh=mesh,
        in_specs=placed,
        out_specs=(P("dom", None), P(None, "dom")),
        check_vma=False,
    )
```

profile of v0, /device:TPU:1, one launch (start us, length us, event | category | flops | bytes accessed | tf_op | source)
XLA Modules:
  0.0 437.3 jit_solution(2807490568553773893)
XLA Ops:
  7.2 0.0 copy-start
  7.2 0.0 all-reduce.6.cloned.1.call-start
  7.2 20.3 %sine_convert_fusion = (bf16[4096,256]{1,0:T(8,128)(2,1)S(1)}, bf16[4096,256]{1,0:T(8,128)(2,1)S(1)}) fusion(f32[3,4096]{1,0:T(4,128)} %param.7, s32[3,256]{1,0:T(4,128)} %param.11), kind=kOutput, calls=%fused_computation.20 | convolution fusion | flops 40895232 | bytes 4246528 | tf_op jit(solution)/shard_map/dot_general | solution.py:13
  27.5 0.0 copy-start.1
  27.5 0.0 copy-start.4
  27.5 0.0 copy-done
  27.5 0.0 copy-start.8
  27.6 0.0 copy-start.12
  27.6 0.0 copy-start.14
  27.6 1.5 fusion.28
  29.0 1.7 copy-done.8
  30.7 0.0 copy-done.12
  30.7 0.0 copy-done.14
  30.7 1.9 fusion.7
  32.6 0.0 copy-done.1
  32.6 0.0 copy-start.6
  32.7 1.5 fusion.26
  34.1 1.5 fusion.27
  35.6 0.0 copy-done.4
  35.6 0.0 copy-done.6
  35.6 0.0 copy-start.11
  35.6 0.0 copy-start.13
  35.6 1.5 fusion.24
  37.0 0.0 all-reduce.6.cloned.1.call-update
  37.1 0.2 all-reduce.4.cloned.1.call-start
  37.3 0.0 copy-done.11
  37.3 272.1 %all-reduce.6.cloned.1.call-done = (f32[256,256]{1,0:T(8,128)}, f32[256,256]{1,0:T(8,128)}, f32[256,256]{1,0:T(8,128)}, f32[256,256]{1,0:T(8,128)}) async-done(((f32[256,256]{1,0:T(8,128)}, f32[256,256]{1,0:T(8,128)}, f32[256,256]{1,0:T(8,128)}, f32[256,256]{1,0:T(8,128)}), (f32[256,256]{1,0:T(8,128)}, f32[256,256]{1,0:T(8,128)}, f32[256,256]{1,0:T(8,128)}, ...) | async-done | bytes 1048592 | tf_op jit(solution)/shard_map/psum | solution.py:82
  309.4 0.0 copy-done.13
  309.4 1.5 multiply_convert_fusion.2
  311.0 0.0 copy-start.2
  311.0 2.4 fusion.25
  313.4 0.0 copy-done.2
  313.4 2.7 convolution_add_fusion
  316.1 0.0 all-reduce.4.cloned.1.call-update
  316.1 0.0 copy-start.3
  316.1 0.0 copy-start.7
  316.2 0.0 copy-start.10
  316.2 2.5 fusion.6
  318.7 0.0 copy-done.3
  318.7 0.3 copy-done.7
  319.0 0.0 copy-done.10
  319.0 0.0 copy-start.5
  319.0 0.7 convolution_multiply_fusion.1
  319.8 0.8 copy-done.5
  320.6 0.0 copy-start.9
  320.6 0.9 fusion.5
  321.5 0.0 copy-done.9
  321.5 1.0 fusion.2
  322.5 3.6 fusion.8
  326.1 31.7 %psum.47 = f32[3,4096]{1,0:T(4,128)} all-reduce(f32[3,4096]{1,0:T(4,128)S(1)} %fusion.8), channel_id=1, replica_groups=mesh['dom'=32,'ka'=8] {'ka'}, use_global_device_ids=true, to_apply=%region_6.0 | all-reduce | flops 12288 | bytes 98304 | tf_op jit(solution)/shard_map/psum | solution.py:92
  357.8 67.9 %all-reduce.4.cloned.1.call-done = f32[4096,256]{1,0:T(8,128)} async-done(((f32[4096,256]{1,0:T(8,128)}), f32[4096,256]{1,0:T(8,128)}) %all-reduce.4.cloned.1.call-update) | async-done | bytes 4194320 | tf_op jit(solution)/shard_map/psum | solution.py:92
  425.7 4.7 %fusion.9 = bf16[4096,256]{1,0:T(8,128)(2,1)} fusion(bf16[4096,256]{1,0:T(8,128)(2,1)} %param.9, f32[4096,256]{1,0:T(8,128)} %all-reduce.4.cloned.1.call-done), kind=kLoop, calls=%fused_computation.18 | loop fusion | flops 4194304 | bytes 8388608 | tf_op jit(solution)/shard_map/convert_element_type | solution.py:93
  (3 shorter events, 0.0 us)
Async XLA Ops:
  7.2 20.4 %copy-start = (bf16[4096,256]{1,0:T(8,128)(2,1)S(1)}, bf16[4096,256]{1,0:T(8,128)(2,1)}, u32[]{:S(2)}) copy-start(bf16[4096,256]{1,0:T(8,128)(2,1)} %param.10) | copy-start | bytes 6291460
  7.2 302.2 %all-reduce.6.cloned.1.call-start = ((), (), s32[]{:S(2)}) async-start(), calls=%async_computation.1 | async-start | bytes 2097152 | tf_op jit(solution)/shard_map/psum | solution.py:82
  27.5 5.1 %copy-start.1 = (bf16[4096,256]{1,0:T(8,128)(2,1)}, bf16[4096,256]{1,0:T(8,128)(2,1)S(1)}, u32[]{:S(2)}) copy-start(bf16[4096,256]{1,0:T(8,128)(2,1)S(1)} %get-tuple-element.6) | copy-start | bytes 6291460
  27.5 8.1 %copy-start.4 = (bf16[4096,256]{1,0:T(8,128)(2,1)}, bf16[4096,256]{1,0:T(8,128)(2,1)S(1)}, u32[]{:S(2)}) copy-start(bf16[4096,256]{1,0:T(8,128)(2,1)S(1)} %get-tuple-element.7) | copy-start | bytes 6291460
  27.5 3.2 copy-start.8
  27.6 3.2 copy-start.12
  27.6 3.1 copy-start.14
  32.6 2.9 copy-start.6
  35.6 1.7 copy-start.11
  35.6 273.8 %copy-start.13 = (f32[16,256]{1,0:T(8,128)S(1)}, f32[16,256]{1,0:T(8,128)}, u32[]{:S(2)}) copy-start(f32[16,256]{1,0:T(8,128)} %param.13) | copy-start | bytes 49156
  37.1 388.6 %all-reduce.4.cloned.1.call-start = ((), (), s32[]{:S(2)}) async-start(), calls=%async_computation | async-start | bytes 8388608 | tf_op jit(solution)/shard_map/psum | solution.py:92
  311.0 2.5 copy-start.2
  316.1 2.5 copy-start.3
  316.1 2.8 copy-start.7
  316.2 2.8 copy-start.10
  319.0 1.6 copy-start.5
  320.6 0.9 copy-start.9
Sparse Core Ops, SparseCore 0:
  37.2 272.1 all-reduce.5
  316.3 109.3 all-reduce.3
where the time goes:
time: 438 us; the launch traced here: 437 us
  waiting for transfers between devices  340 us (78%)
  matrix products  43.4 us (10%)
  blocking collectives  31.7 us (7%)
  between operations  14.2 us (3%)
  other arithmetic  4.77 us (1%)
    psum x1, waiting for transfers between devices, body(): sr, si, gr, gi = lax.psum((terms[0], terms[1], terms[2], terms[3]), 'dom')  272 us
    psum x1, waiting for transfers between devices, body(): total, forces = lax.psum((message_part, force_part), 'ka')  67.9 us
    psum x1, blocking collectives, body(): total, forces = lax.psum((message_part, force_part), 'ka')  31.7 us
    dot_general x1, matrix products, phase_tables(): lax.dot_general(frac, miller.astype(jnp.float32), (((0,), (0,)), ((), ())...  20.3 us
  transfers between devices with their start and end apart: 2, of which 2 were waited for; matrix products, arithmetic and copies ran while one was open for 2% of the time, Pallas kernels for 0%

commit v1 on v0

v1 whole, which is shorter than its diff:
```python
import functools
import math

import jax
import jax.numpy as jnp
from jax import lax
from jax.experimental import pallas as pl
from jax.experimental.pallas import tpu as pltpu
from jax.sharding import Mesh, PartitionSpec as P

TWO_PI = 6.283185307179586
BOX = 64.0
MIB = 1024 * 1024
SINE = (4.4428679, -7.30744342, 3.59478803, -0.7843739)
COSINE = (1.41420408, -6.97764207, 5.71523842, -1.72834863)
OVER = ("xh", "z")
ACROSS = ("xl", "y")
SWAP = [(0, 1), (1, 0)]


def triple(x):
    hi = x.astype(jnp.bfloat16)
    rest = x - hi.astype(jnp.float32)
    mid = rest.astype(jnp.bfloat16)
    low = (rest - mid.astype(jnp.float32)).astype(jnp.bfloat16)
    return jnp.concatenate([hi, mid, low], axis=0)


def contract(left, right, dims):
    return lax.dot_general(left, right, (dims, ((), ())), preferred_element_type=jnp.float32)


def cos_sin(turns):
    r = turns - jnp.round(turns)
    t = r * r
    s = (((SINE[3] * t + SINE[2]) * t + SINE[1]) * t + SINE[0]) * r
    c = ((COSINE[3] * t + COSINE[2]) * t + COSINE[1]) * t + COSINE[0]
    return 1.0 - s * s, s * c


def factors_kernel(frac, species, feats, cot, miller, gain, emb, tab, part, acc, turns):
    step = pl.program_id(0)
    kn = miller.shape[1]
    mill = miller[...].astype(jnp.float32).astype(jnp.bfloat16)
    mill3 = jnp.concatenate([mill, mill, mill], axis=0)
    turns[...] = contract(mill3, triple(frac[...]), ((0,), (0,)))
    kinds = gain.shape[0]
    onehot = (lax.broadcasted_iota(jnp.int32, (kinds, species.shape[1]), 0) == species[...]).astype(jnp.float32)
    onehot = onehot.astype(jnp.bfloat16)
    onehot3 = jnp.concatenate([onehot, onehot, onehot], axis=0)
    gains = contract(onehot3, triple(gain[...]), ((0,), (0,)))
    rows = (feats[...].astype(jnp.float32) * gains).astype(jnp.bfloat16)
    emb[...] = rows

    def chunk(i, _):
        at = pl.ds(pl.multiple_of(i * 16, 16), 16)
        c, s = cos_sin(turns[at, :])
        tab[at, :] = c.astype(jnp.bfloat16)
        tab[pl.ds(pl.multiple_of(kn + i * 16, 16), 16), :] = s.astype(jnp.bfloat16)
        return 0

    lax.fori_loop(0, kn // 16, chunk, 0, unroll=4)

    @pl.when(step == 0)
    def _():
        acc[...] = jnp.zeros_like(acc)

    both = jnp.concatenate([rows, cot[...]], axis=1)
    acc[...] += contract(tab[...], both, ((1,), (0,)))

    @pl.when(step == pl.num_programs(0) - 1)
    def _():
        part[...] = acc[...].astype(jnp.bfloat16)


def factors(frac, species, feats, cot, miller, gain, tile=512):
    n, ch = feats.shape
    kn = miller.shape[1]
    return pl.pallas_call(
        factors_kernel,
        grid=(n // tile,),
        in_specs=[
            pl.BlockSpec((3, tile), lambda i: (0, i)),
            pl.BlockSpec((1, tile), lambda i: (0, i)),
            pl.BlockSpec((tile, ch), lambda i: (i, 0)),
            pl.BlockSpec((tile, ch), lambda i: (i, 0)),
            pl.BlockSpec((3, kn), lambda i: (0, 0)),
            pl.BlockSpec(gain.shape, lambda i: (0, 0)),
        ],
        out_specs=[
            pl.BlockSpec((tile, ch), lambda i: (i, 0)),
            pl.BlockSpec((2 * kn, tile), lambda i: (0, i)),
            pl.BlockSpec((2 * kn, 2 * ch), lambda i: (0, 0)),
        ],
        out_shape=[
            jax.ShapeDtypeStruct((n, ch), jnp.bfloat16),
            jax.ShapeDtypeStruct((2 * kn, n), jnp.bfloat16),
            jax.ShapeDtypeStruct((2 * kn, 2 * ch), jnp.bfloat16),
        ],
        scratch_shapes=[
            pltpu.VMEM((2 * kn, 2 * ch), jnp.float32),
            pltpu.VMEM((kn, tile), jnp.float32),
        ],
        compiler_params=pltpu.CompilerParams(vmem_limit_bytes=16 * MIB),
        cost_estimate=pl.CostEstimate(flops=8 * n * kn * ch, bytes_accessed=8 * n * ch + 4 * n * kn, transcendentals=0),
        name="factors",
    )(frac, species, feats, cot, miller, gain)


def tables_kernel(frac, mill, cos, sin, turns):
    turns[...] = contract(triple(frac[...]), mill[...], ((0,), (0,)))

    def chunk(i, _):
        at = pl.ds(pl.multiple_of(i * 16, 16), 16)
        c, s = cos_sin(turns[at, :])
        cos[at, :] = c.astype(jnp.bfloat16)
        sin[at, :] = s.astype(jnp.bfloat16)
        return 0

    lax.fori_loop(0, turns.shape[0] // 16, chunk, 0, unroll=4)


def tables(frac, mill, tile=512, wide=512):
    n = frac.shape[1]
    kn = mill.shape[1]
    return pl.pallas_call(
        tables_kernel,
        grid=(n // tile, kn // wide),
        in_specs=[
            pl.BlockSpec((3, tile), lambda i, j: (0, i)),
            pl.BlockSpec((mill.shape[0], wide), lambda i, j: (0, j)),
        ],
        out_specs=[pl.BlockSpec((tile, wide), lambda i, j: (i, j))] * 2,
        out_shape=[jax.ShapeDtypeStruct((n, kn), jnp.bfloat16)] * 2,
        scratch_shapes=[pltpu.VMEM((tile, wide), jnp.float32)],
        compiler_params=pltpu.CompilerParams(vmem_limit_bytes=8 * MIB),
        cost_estimate=pl.CostEstimate(flops=20 * n * kn * 200, bytes_accessed=4 * n * kn, transcendentals=0),
        name="tables",
    )(frac, mill)


def forces_kernel(scale, tab, cot, emb, panel, mill, out, work):
    kn = mill.shape[0]
    both = jnp.concatenate([cot[...], emb[...]], axis=1)
    work[...] = contract(panel[...], both, ((1,), (1,)))

    def chunk(i, sums):
        at = pl.ds(pl.multiple_of(i * 16, 16), 16)
        at2 = pl.ds(pl.multiple_of(kn + i * 16, 16), 16)
        c = tab[at, :].astype(jnp.float32)
        s = tab[at2, :].astype(jnp.float32)
        grads = c * work[at2, :] - s * work[at, :]
        m = mill[at, :]
        return tuple(total + m[:, d:d + 1] * grads for d, total in enumerate(sums))

    zero = jnp.zeros((16, tab.shape[1]), jnp.float32)
    sums = lax.fori_loop(0, kn // 16, chunk, (zero, zero, zero), unroll=2)
    out[...] = jnp.concatenate([jnp.sum(total, axis=0, keepdims=True) for total in sums], axis=0) * scale


def forces_of(tab, cot, emb, panel, mill, scale, tile=512):
    n, ch = cot.shape
    kn = mill.shape[0]
    return pl.pallas_call(
        functools.partial(forces_kernel, scale),
        grid=(n // tile,),
        in_specs=[
            pl.BlockSpec((2 * kn, tile), lambda i: (0, i)),
            pl.BlockSpec((tile, ch), lambda i: (i, 0)),
            pl.BlockSpec((tile, ch), lambda i: (i, 0)),
            pl.BlockSpec((2 * kn, 2 * ch), lambda i: (0, 0)),
            pl.BlockSpec(mill.shape, lambda i: (0, 0)),
        ],
        out_specs=pl.BlockSpec((3, tile), lambda i: (0, i)),
        out_shape=jax.ShapeDtypeStruct((3, n), jnp.float32),
        scratch_shapes=[pltpu.VMEM((2 * kn, tile), jnp.float32)],
        compiler_params=pltpu.CompilerParams(vmem_limit_bytes=16 * MIB),
        cost_estimate=pl.CostEstimate(flops=8 * n * kn * ch, bytes_accessed=4 * n * kn + 4 * n * ch, transcendentals=0),
        name="forces",
    )(tab, cot, emb, panel, mill)


def message_kernel(scale, cos, sin, real, imag, feats, out):
    total = contract(cos[...], real[...], ((1,), (0,))) + contract(sin[...], imag[...], ((1,), (0,)))
    out[...] = (feats[...].astype(jnp.float32) + total * scale).astype(jnp.bfloat16)


def message(cos, sin, real, imag, feats, scale, tile=512):
    n, ch = feats.shape
    kn = real.shape[0]
    return pl.pallas_call(
        functools.partial(message_kernel, scale),
        grid=(n // tile,),
        in_specs=[
            pl.BlockSpec((tile, kn), lambda i: (i, 0)),
            pl.BlockSpec((tile, kn), lambda i: (i, 0)),
            pl.BlockSpec((kn, ch), lambda i: (0, 0)),
            pl.BlockSpec((kn, ch), lambda i: (0, 0)),
            pl.BlockSpec((tile, ch), lambda i: (i, 0)),
        ],
        out_specs=pl.BlockSpec((tile, ch), lambda i: (i, 0)),
        out_shape=jax.ShapeDtypeStruct((n, ch), jnp.bfloat16),
        compiler_params=pltpu.CompilerParams(vmem_limit_bytes=24 * MIB),
        cost_estimate=pl.CostEstimate(flops=4 * n * kn * ch, bytes_accessed=4 * n * kn + 4 * n * ch, transcendentals=0),
        name="message",
    )(cos, sin, real, imag, feats)


def weights_of(mills, filter_weight):
    length = jnp.sqrt(jnp.sum(mills * mills, axis=0))
    count = filter_weight.shape[0]
    centres = jnp.arange(count, dtype=jnp.float32) * (14.0 / (count - 1))
    basis = jnp.exp(-((length[:, None] - centres[None, :]) ** 2))
    return jnp.dot(basis, filter_weight, precision=lax.Precision.HIGHEST)


def everyone(x, axes):
    n = lax.axis_size(axes)
    return lax.all_to_all(jnp.broadcast_to(x[None], (n,) + x.shape), axes, 0, 0)


def body(frac, species, feats, cot, miller, gain, filter_weight):
    n, ch = feats.shape
    kn = miller.shape[1]
    inv_n = 1.0 / math.sqrt(n * lax.axis_size(("xh", "z", "core")))
    inv_k = 1.0 / math.sqrt(kn * lax.axis_size(ACROSS))
    groups = lax.axis_size(OVER)
    rows = kn // groups
    core = lax.axis_index("core")

    mills = miller.astype(jnp.float32)
    mill_all = everyone(jnp.concatenate([mills] * 3, axis=0).astype(jnp.bfloat16), ACROSS)
    mill_all = mill_all.transpose(1, 0, 2).reshape(9, -1)

    emb, tab, part = factors(frac, species.reshape(1, n), feats, cot, miller, gain)
    cos, sin = tables(frac, mill_all)

    mine = lax.dynamic_slice_in_dim(mills, lax.axis_index(OVER) * rows, rows, axis=1)
    weights = weights_of(mine, filter_weight) * inv_n

    halves = part.reshape(2, kn, 2 * ch)
    keep = lax.dynamic_index_in_dim(halves, core, 0, keepdims=False)
    give = lax.dynamic_index_in_dim(halves, 1 - core, 0, keepdims=False)
    got = lax.ppermute(give, "core", SWAP)
    pair = (keep.astype(jnp.float32) + got.astype(jnp.float32)).astype(jnp.bfloat16)
    spread = lax.all_to_all(pair.reshape(groups, rows, 2 * ch), OVER, 0, 0)
    total = jnp.sum(spread.astype(jnp.float32), axis=0)
    panel = (total * jnp.concatenate([weights, weights], axis=1)).astype(jnp.bfloat16)
    panel = everyone(panel, OVER).reshape(kn, 2 * ch)

    everywhere = everyone(panel[:, :ch], ACROSS).reshape(-1, ch)
    other = lax.ppermute(panel, "core", SWAP)
    first = core == 0
    local = jnp.concatenate([jnp.where(first, panel, other), jnp.where(first, other, panel)], axis=0)
    force = forces_of(tab, cot, emb, local, mills.T, -TWO_PI / BOX * inv_k)
    force_all = everyone(force, ACROSS)
    forces = jnp.sum(force_all, axis=0)

    other = lax.ppermute(everywhere, "core", SWAP)
    real = jnp.where(first, everywhere, other)
    imag = jnp.where(first, other, everywhere)
    updated = message(cos, sin, real, imag, feats, inv_k)
    return updated, forces


def solution(mesh):
    sizes = dict(mesh.shape)
    fine = Mesh(mesh.devices.reshape(2, sizes["dom"] // 4, 2, 2, sizes["ka"] // 2), ("xh", "z", "core", "xl", "y"))
    dom = ("xh", "z", "core")
    placed = (P(None, dom), P(dom), P(dom, None), P(dom, None), P(None, ACROSS), P(), P())
    return jax.shard_map(
        body,
        mesh=fine,
        in_specs=placed,
        out_specs=(P(dom, None), P(None, dom)),
        check_vma=False,
    )
```

time: 438 us -> 173 us (0.39)
  waiting for transfers between devices: 340 us -> 26.2 us
  Pallas kernels: 0 us -> 70.9 us
  matrix products: 43.4 us -> 0.2 us
  starting transfers between devices: 0.26 us -> 36.3 us
  blocking collectives: 31.7 us -> 0 us
  local copies, waits for them, and re-layouts: 2.95 us -> 34.6 us
  between operations: 14.2 us -> 0.88 us
    psum x2 -> x0, waiting for transfers between devices: 340 us -> none  [the longest x1 272 us: body(): sr, si, gr, gi = lax.psum((terms[0], terms[1], terms[2], terms[3]), 'dom')]
    pallas_call x0 -> x4, Pallas kernels: none -> 70.9 us  [the longest x1 37.5 us: tables(): pl.pallas_call(tables_kernel, grid=(n // tile, kn // wide), in_specs=[pl....]
    dot_general x14 -> x1, matrix products: 43.4 us -> 0.2 us  [weights_of(): return jnp.dot(basis, filter_weight, precision=lax.Precision.HIGHEST)]
    psum x1 -> x0, blocking collectives: 31.7 us -> none  [body(): total, forces = lax.psum((message_part, force_part), 'ka')]
    all_to_all x0 -> x5, starting transfers between devices: none -> 27.7 us  [the longest x4 18.7 us: everyone(): return lax.all_to_all(jnp.broadcast_to(x[None], (n,) + x.shape), axes, 0, 0)]
    unnamed x30 -> x38, local copies, waits for them, and re-layouts: 2.95 us -> 30.2 us
    all_to_all x0 -> x5, waiting for transfers between devices: none -> 23.8 us  [the longest x4 13.7 us: everyone(): return lax.all_to_all(jnp.broadcast_to(x[None], (n,) + x.shape), axes, 0, 0)]
    ppermute x0 -> x3, starting transfers between devices: none -> 8.61 us  [the longest x1 4.64 us: body(): other = lax.ppermute(panel, 'core', SWAP)]
  transfers between devices with their start and end apart: 2 -> 8, of which waited for: 2 -> 5; matrix products, arithmetic and copies ran while one was open for 2% -> 2% of each run, Pallas kernels for 0% -> 28%
where the time goes in v1:
time: 173 us; the launch traced here: 172 us
  Pallas kernels  70.9 us (41%)
  starting transfers between devices  36.3 us (21%)
  local copies, waits for them, and re-layouts  34.6 us (20%)
  waiting for transfers between devices  26.2 us (15%)
  other arithmetic  2.97 us (2%)
    pallas_call x1, Pallas kernels, tables(): pl.pallas_call(tables_kernel, grid=(n // tile, kn // wide), in_specs=[pl....  37.5 us
    unnamed x38, local copies, waits for them, and re-layouts  30.2 us
    all_to_all x4, starting transfers between devices, everyone(): return lax.all_to_all(jnp.broadcast_to(x[None], (n,) + x.shape), axes, 0, 0)  18.7 us
    pallas_call x1, Pallas kernels, message(): pl.pallas_call(functools.partial(message_kernel, scale), grid=(n // tile,...  13.9 us
    all_to_all x4, waiting for transfers between devices, everyone(): return lax.all_to_all(jnp.broadcast_to(x[None], (n,) + x.shape), axes, 0, 0)  13.7 us
    all_to_all x1, waiting for transfers between devices, body(): spread = lax.all_to_all(pair.reshape(groups, rows, 2 * ch), OVER, 0, 0)  10.1 us
    pallas_call x1, Pallas kernels, forces_of(): pl.pallas_call(functools.partial(forces_kernel, scale), grid=(n // tile,)...  9.93 us
    pallas_call x1, Pallas kernels, factors(): pl.pallas_call(factors_kernel, grid=(n // tile,), in_specs=[pl.BlockSpec(...  9.61 us
  transfers between devices with their start and end apart: 8, of which 5 were waited for; matrix products, arithmetic and copies ran while one was open for 2% of the time, Pallas kernels for 28%

profile of v1, /device:TPU:1, one launch (start us, length us, event | category | flops | bytes accessed | tf_op | source)
XLA Modules:
  0.0 172.1 jit_solution(6376254885093223624)
XLA Ops:
  0.6 0.0 copy-start
  0.7 0.0 copy-start.6
  0.7 1.6 copy-done.6
  2.2 0.0 copy-start.8
  2.2 1.6 copy-done.8
  3.8 0.0 copy-start.12
  3.8 0.7 copy-done.12
  4.5 0.0 copy-start.14
  4.5 0.8 copy-done.14
  5.4 0.0 copy-start.16
  5.4 0.7 copy-done.16
  6.1 0.0 copy-start.17
  6.1 0.7 copy-done.17
  6.8 0.0 copy-start.13
  6.8 9.6 %factors.1 = (bf16[4096,256]{1,0:T(8,128)(2,1)S(1)}, bf16[512,4096]{1,0:T(8,128)(2,1)S(1)}, bf16[512,512]{1,0:T(8,128)(2,1)S(1)}) custom-call(f32[3,4096]{1,0:T(4,128)S(1)} %copy-done.14, s32[1,4096]{1,0:T(1,128)S(1)} %bitcast.24, bf16[4096,256]{1,0:T(8,128)(2,1)S(1)} %copy-done.8, bf16[4096,256]{1,0:T(8,128)(2,1)S(1)} %copy-done.6, ...), custom_call_target="tpu_custom_call" | custom-call | flops 2147483648 | bytes 12582912 | tf_op jit(solution)/shard_map/factors/pallas_call | solution.py:79
  16.4 0.0 copy-start.4
  16.4 1.9 %copy-done.4 = bf16[512,4096]{1,0:T(8,128)(2,1)} copy-done((bf16[512,4096]{1,0:T(8,128)(2,1)}, bf16[512,4096]{1,0:T(8,128)(2,1)S(1)}, u32[]{:S(2)}) %copy-start.4) | copy-done | bytes 4194328
  18.4 1.3 copy-done.10
  19.7 3.3 %collective-permute-start = (bf16[256,512]{1,0:T(8,128)(2,1)S(1)}, bf16[256,512]{1,0:T(8,128)(2,1)S(1)}, u32[]{:S(2)}, u32[]{:S(2)}) collective-permute-start(bf16[256,512]{1,0:T(8,128)(2,1)S(1)} %dynamic-slice_bitcast_fusion), channel_id=1, source_target_pairs={{0,8},{8,0},{1,9},{9,1},{2,10},{10,2},{3,11},{11,3},{4,12},{12,4},... | collective-permute-start | bytes 786440 | tf_op jit(solution)/shard_map/ppermute | solution.py:244
  23.0 1.2 collective-permute-done
  24.2 0.8 fusion
  25.0 9.0 %all-to-all-start.1 = ((bf16[16,16,512]{2,1,0:T(8,128)(2,1)}), bf16[16,16,512]{2,1,0:T(8,128)(2,1)S(1)}, u32[]{:S(2)}, u32[]{:S(2)}) async-start(bf16[16,16,512]{2,1,0:T(8,128)(2,1)} %bitcast.5), calls=%async_computation.1 | async-start | bytes 524288 | tf_op jit(solution)/shard_map/all_to_all | solution.py:246
  34.0 0.0 copy-done.13
  34.0 0.1 multiply_reduce_fusion
  34.1 0.0 copy-done
  34.1 0.2 convolution_multiply_fusion
  34.3 10.1 %all-to-all-done.1 = bf16[16,16,512]{2,1,0:T(8,128)(2,1)S(1)} async-done(((bf16[16,16,512]{2,1,0:T(8,128)(2,1)}), bf16[16,16,512]{2,1,0:T(8,128)(2,1)S(1)}, u32[]{:S(2)}, u32[]{:S(2)}) %all-to-all-start.1) | async-done | bytes 262176 | tf_op jit(solution)/shard_map/all_to_all | solution.py:246
  44.5 0.7 broadcast_in_dim.9
  45.2 5.5 %all-to-all-start.2 = ((bf16[16,16,512]{2,1,0:T(8,128)(2,1)}), bf16[16,16,512]{2,1,0:T(8,128)(2,1)}, u32[]{:S(2)}, u32[]{:S(2)}) async-start(bf16[16,16,512]{2,1,0:T(8,128)(2,1)} %broadcast_in_dim.9), calls=%async_computation.2 | async-start | bytes 524288 | tf_op jit(solution)/shard_map/all_to_all | solution.py:219
  50.7 9.4 %all-to-all-done.2 = bf16[16,16,512]{2,1,0:T(8,128)(2,1)} async-done(((bf16[16,16,512]{2,1,0:T(8,128)(2,1)}), bf16[16,16,512]{2,1,0:T(8,128)(2,1)}, u32[]{:S(2)}, u32[]{:S(2)}) %all-to-all-start.2) | async-done | bytes 262176 | tf_op jit(solution)/shard_map/all_to_all | solution.py:219
  60.1 0.6 broadcast_in_dim.8
  60.8 4.2 %all-to-all-start = ((bf16[8,9,256]{2,1,0:T(8,128)(2,1)}), bf16[8,9,256]{2,1,0:T(8,128)(2,1)S(1)}, u32[]{:S(2)}, u32[]{:S(2)}) async-start(bf16[8,9,256]{2,1,0:T(8,128)(2,1)} %broadcast_in_dim.8), calls=%async_computation | async-start | bytes 131072 | tf_op jit(solution)/shard_map/all_to_all | solution.py:219
  65.0 0.9 slice.4
  65.9 4.3 %all-to-all-done = bf16[8,9,256]{2,1,0:T(8,128)(2,1)S(1)} async-done(((bf16[8,9,256]{2,1,0:T(8,128)(2,1)}), bf16[8,9,256]{2,1,0:T(8,128)(2,1)S(1)}, u32[]{:S(2)}, u32[]{:S(2)}) %all-to-all-start) | async-done | bytes 36896 | tf_op jit(solution)/shard_map/all_to_all | solution.py:219
  70.2 1.1 broadcast_in_dim.10
  71.2 0.0 copy-start.7
  71.2 3.7 %all-to-all-start.3 = ((bf16[8,256,256]{2,1,0:T(8,128)(2,1)}), bf16[8,256,256]{2,1,0:T(8,128)(2,1)S(1)}, u32[]{:S(2)}, u32[]{:S(2)}) async-start(bf16[8,256,256]{2,1,0:T(8,128)(2,1)} %broadcast_in_dim.10), calls=%async_computation.3 | async-start | bytes 2097152 | tf_op jit(solution)/shard_map/all_to_all | solution.py:219
  74.9 4.6 %collective-permute-start.2 = (bf16[256,512]{1,0:T(8,128)(2,1)}, bf16[256,512]{1,0:T(8,128)(2,1)}, u32[]{:S(2)}, u32[]{:S(2)}) collective-permute-start(bf16[256,512]{1,0:T(8,128)(2,1)} %bitcast.6), channel_id=1, source_target_pairs={{0,8},{8,0},{1,9},{9,1},{2,10},{10,2},{3,11},{11,3},{4,12},{12,4},... | collective-permute-start | bytes 786440 | tf_op jit(solution)/shard_map/ppermute | solution.py:252
  79.6 0.1 copy.28
  79.7 0.0 copy-start.11
  79.8 1.3 collective-permute-done.2
  81.1 1.1 broadcast_select_fusion.3
  82.2 0.0 copy-done.7
  82.2 0.0 copy-done.11
  82.2 0.0 copy-start.5
  82.2 2.2 %copy-done.5 = bf16[512,4096]{1,0:T(8,128)(2,1)S(1)} copy-done((bf16[512,4096]{1,0:T(8,128)(2,1)S(1)}, bf16[512,4096]{1,0:T(8,128)(2,1)}, u32[]{:S(2)}) %copy-start.5) | copy-done | bytes 4194328
  84.4 0.0 copy-start.15
  84.4 9.9 %forces.1 = f32[3,4096]{1,0:T(4,128)S(1)} custom-call(bf16[512,4096]{1,0:T(8,128)(2,1)S(1)} %copy-done.5, bf16[4096,256]{1,0:T(8,128)(2,1)S(1)} %copy-done.7, bf16[4096,256]{1,0:T(8,128)(2,1)S(1)} %copy-done.11, bf16[512,512]{1,0:T(8,128)(2,1)S(1)} %pad_maximum_fusion.panel, f32[256,3]{1,0:T(8,128)S(1)} %bitcast.20), custom_call_target="tpu_custom_call" | custom-call | flops 2147483648 | bytes 8388608 | tf_op jit(solution)/shard_map/forces/pallas_call | solution.py:164
  94.4 0.0 all-to-all-done.3
  94.4 0.9 broadcast_in_dim.11
  95.2 5.3 %all-to-all-start.4 = ((f32[8,3,4096]{2,1,0:T(4,128)}), f32[8,3,4096]{2,1,0:T(4,128)S(1)}, u32[]{:S(2)}, u32[]{:S(2)}) async-start(f32[8,3,4096]{2,1,0:T(4,128)} %broadcast_in_dim.11), calls=%async_computation.4 | async-start | bytes 1048576 | tf_op jit(solution)/shard_map/all_to_all | solution.py:219
  100.5 0.7 collective-permute-start.1
  101.1 0.0 copy-done.15
  101.1 37.5 %tables.1 = (bf16[4096,2048]{1,0:T(8,128)(2,1)S(1)}, bf16[4096,2048]{1,0:T(8,128)(2,1)S(1)}) custom-call(f32[3,4096]{1,0:T(4,128)S(1)} %copy-done.15, bf16[9,2048]{1,0:T(8,128)(2,1)S(1)} %bitcast.23), custom_call_target="tpu_custom_call" | custom-call | flops 33554432000 | bytes 33554432 | tf_op jit(solution)/shard_map/tables/pallas_call | solution.py:126
  138.6 0.0 copy-start.1
  138.6 5.7 %copy-done.1 = bf16[4096,2048]{1,0:T(8,128)(2,1)} copy-done((bf16[4096,2048]{1,0:T(8,128)(2,1)}, bf16[4096,2048]{1,0:T(8,128)(2,1)S(1)}, u32[]{:S(2)}) %copy-start.1) | copy-done | bytes 16777240
  144.3 5.7 %copy-done.3 = bf16[4096,2048]{1,0:T(8,128)(2,1)} copy-done((bf16[4096,2048]{1,0:T(8,128)(2,1)}, bf16[4096,2048]{1,0:T(8,128)(2,1)S(1)}, u32[]{:S(2)}) %copy-start.3) | copy-done | bytes 16777240
  150.1 0.0 all-to-all-done.4
  150.1 0.7 reduce_sum.29
  150.8 0.0 collective-permute-done.1
  150.8 0.2 broadcast_select_fusion
  151.0 1.4 copy-done.9
  152.4 5.8 %copy-done.2 = bf16[4096,2048]{1,0:T(8,128)(2,1)S(1)} copy-done((bf16[4096,2048]{1,0:T(8,128)(2,1)S(1)}, bf16[4096,2048]{1,0:T(8,128)(2,1)}, u32[]{:S(2)}) %copy-start.2) | copy-done | bytes 16777240
  158.2 13.9 %message.1 = bf16[4096,256]{1,0:T(8,128)(2,1)} custom-call(bf16[4096,2048]{1,0:T(8,128)(2,1)S(1)} %copy-done.2, bf16[4096,2048]{1,0:T(8,128)(2,1)} %copy-done.3, bf16[2048,256]{1,0:T(8,128)(2,1)S(1)} %get-tuple-element.13.real, bf16[2048,256]{1,0:T(8,128)(2,1)S(1)} %get-tuple-element.12.imag, bf16[4096,256]{1,0:T(8,128)(2,1)S(1)} %copy-done.9), custom_call_target="tpu_custom_call" | custom-call | flops 8589934592 | bytes 37748736 | tf_op jit(solution)/shard_map/message/pallas_call | solution.py:191
  (15 shorter events, 0.2 us)
Async XLA Ops:
  0.6 33.5 %copy-start = (f32[16,256]{1,0:T(8,128)S(1)}, f32[16,256]{1,0:T(8,128)}, u32[]{:S(2)}) copy-start(f32[16,256]{1,0:T(8,128)} %param.13) | copy-start | bytes 49156
  0.7 1.6 copy-start.6
  2.2 1.6 copy-start.8
  3.8 0.7 copy-start.12
  4.5 0.8 copy-start.14
  5.4 0.7 copy-start.16
  6.1 0.7 copy-start.17
  6.8 27.2 %copy-start.13 = (s32[3,256]{1,0:T(4,128)S(1)}, s32[3,256]{1,0:T(4,128)}, u32[]{:S(2)}) copy-start(s32[3,256]{1,0:T(4,128)} %miller.1) | copy-start | bytes 9220
  16.4 2.0 %copy-start.4 = (bf16[512,4096]{1,0:T(8,128)(2,1)}, bf16[512,4096]{1,0:T(8,128)(2,1)S(1)}, u32[]{:S(2)}) copy-start(bf16[512,4096]{1,0:T(8,128)(2,1)S(1)} %get-tuple-element.10.tab) | copy-start | bytes 12582916
  18.4 1.3 copy-start.10
  19.7 4.5 %collective-permute-start = (bf16[256,512]{1,0:T(8,128)(2,1)S(1)}, bf16[256,512]{1,0:T(8,128)(2,1)S(1)}, u32[]{:S(2)}, u32[]{:S(2)}) collective-permute-start(bf16[256,512]{1,0:T(8,128)(2,1)S(1)} %dynamic-slice_bitcast_fusion), channel_id=1, source_target_pairs={{0,8},{8,0},{1,9},{9,1},{2,10},{10,2},{3,11},{11,3},{4,12},{12,4},... | collective-permute-start | bytes 786440 | tf_op jit(solution)/shard_map/ppermute | solution.py:244
  25.0 19.5 %all-to-all-start.1 = ((bf16[16,16,512]{2,1,0:T(8,128)(2,1)}), bf16[16,16,512]{2,1,0:T(8,128)(2,1)S(1)}, u32[]{:S(2)}, u32[]{:S(2)}) async-start(bf16[16,16,512]{2,1,0:T(8,128)(2,1)} %bitcast.5), calls=%async_computation.1 | async-start | bytes 524288 | tf_op jit(solution)/shard_map/all_to_all | solution.py:246
  45.2 14.9 %all-to-all-start.2 = ((bf16[16,16,512]{2,1,0:T(8,128)(2,1)}), bf16[16,16,512]{2,1,0:T(8,128)(2,1)}, u32[]{:S(2)}, u32[]{:S(2)}) async-start(bf16[16,16,512]{2,1,0:T(8,128)(2,1)} %broadcast_in_dim.9), calls=%async_computation.2 | async-start | bytes 524288 | tf_op jit(solution)/shard_map/all_to_all | solution.py:219
  60.8 9.4 %all-to-all-start = ((bf16[8,9,256]{2,1,0:T(8,128)(2,1)}), bf16[8,9,256]{2,1,0:T(8,128)(2,1)S(1)}, u32[]{:S(2)}, u32[]{:S(2)}) async-start(bf16[8,9,256]{2,1,0:T(8,128)(2,1)} %broadcast_in_dim.8), calls=%async_computation | async-start | bytes 131072 | tf_op jit(solution)/shard_map/all_to_all | solution.py:219
  71.2 11.0 %copy-start.7 = (bf16[4096,256]{1,0:T(8,128)(2,1)S(1)}, bf16[4096,256]{1,0:T(8,128)(2,1)}, u32[]{:S(2)}) copy-start(bf16[4096,256]{1,0:T(8,128)(2,1)} %cot.3) | copy-start | bytes 6291460
  71.2 23.1 %all-to-all-start.3 = ((bf16[8,256,256]{2,1,0:T(8,128)(2,1)}), bf16[8,256,256]{2,1,0:T(8,128)(2,1)S(1)}, u32[]{:S(2)}, u32[]{:S(2)}) async-start(bf16[8,256,256]{2,1,0:T(8,128)(2,1)} %broadcast_in_dim.10), calls=%async_computation.3 | async-start | bytes 2097152 | tf_op jit(solution)/shard_map/all_to_all | solution.py:219
  74.9 6.1 %collective-permute-start.2 = (bf16[256,512]{1,0:T(8,128)(2,1)}, bf16[256,512]{1,0:T(8,128)(2,1)}, u32[]{:S(2)}, u32[]{:S(2)}) collective-permute-start(bf16[256,512]{1,0:T(8,128)(2,1)} %bitcast.6), channel_id=1, source_target_pairs={{0,8},{8,0},{1,9},{9,1},{2,10},{10,2},{3,11},{11,3},{4,12},{12,4},... | collective-permute-start | bytes 786440 | tf_op jit(solution)/shard_map/ppermute | solution.py:252
  79.7 2.5 %copy-start.11 = (bf16[4096,256]{1,0:T(8,128)(2,1)S(1)}, bf16[4096,256]{1,0:T(8,128)(2,1)}, u32[]{:S(2)}) copy-start(bf16[4096,256]{1,0:T(8,128)(2,1)} %copy-done.10) | copy-start | bytes 6291460
  82.2 2.2 %copy-start.5 = (bf16[512,4096]{1,0:T(8,128)(2,1)S(1)}, bf16[512,4096]{1,0:T(8,128)(2,1)}, u32[]{:S(2)}) copy-start(bf16[512,4096]{1,0:T(8,128)(2,1)} %copy-done.4) | copy-start | bytes 12582916
  84.4 16.7 %copy-start.15 = (f32[3,4096]{1,0:T(4,128)S(1)}, f32[3,4096]{1,0:T(4,128)}, u32[]{:S(2)}) copy-start(f32[3,4096]{1,0:T(4,128)} %frac.3) | copy-start | bytes 147460
  95.2 54.9 %all-to-all-start.4 = ((f32[8,3,4096]{2,1,0:T(4,128)}), f32[8,3,4096]{2,1,0:T(4,128)S(1)}, u32[]{:S(2)}, u32[]{:S(2)}) async-start(f32[8,3,4096]{2,1,0:T(4,128)} %broadcast_in_dim.11), calls=%async_computation.4 | async-start | bytes 1048576 | tf_op jit(solution)/shard_map/all_to_all | solution.py:219
  100.5 50.3 %collective-permute-start.1 = (bf16[2048,256]{1,0:T(8,128)(2,1)S(1)}, bf16[2048,256]{1,0:T(8,128)(2,1)S(1)}, u32[]{:S(2)}, u32[]{:S(2)}) collective-permute-start(bf16[2048,256]{1,0:T(8,128)(2,1)S(1)} %bitcast.25), channel_id=1, source_target_pairs={{0,8},{8,0},{1,9},{9,1},{2,10},{10,2},{3,11},{11,3},{4,12},{12,4},... | collective-permute-start | bytes 3145736 | tf_op jit(solution)/shard_map/ppermute | solution.py:259
  138.6 5.7 %copy-start.1 = (bf16[4096,2048]{1,0:T(8,128)(2,1)}, bf16[4096,2048]{1,0:T(8,128)(2,1)S(1)}, u32[]{:S(2)}) copy-start(bf16[4096,2048]{1,0:T(8,128)(2,1)S(1)} %get-tuple-element.7.cos) | copy-start | bytes 50331652
  144.3 5.7 %copy-start.3 = (bf16[4096,2048]{1,0:T(8,128)(2,1)}, bf16[4096,2048]{1,0:T(8,128)(2,1)S(1)}, u32[]{:S(2)}) copy-start(bf16[4096,2048]{1,0:T(8,128)(2,1)S(1)} %get-tuple-element.8.sin) | copy-start | bytes 50331652
  150.8 1.6 copy-start.9
  152.4 5.8 %copy-start.2 = (bf16[4096,2048]{1,0:T(8,128)(2,1)S(1)}, bf16[4096,2048]{1,0:T(8,128)(2,1)}, u32[]{:S(2)}) copy-start(bf16[4096,2048]{1,0:T(8,128)(2,1)} %copy-done.1) | copy-start | bytes 50331652

commit v2 on v0

v2 whole, which is shorter than its diff:
```python
import functools
import math

import jax
import jax.numpy as jnp
from jax import lax
from jax.experimental import pallas as pl
from jax.experimental.pallas import tpu as pltpu
from jax.sharding import Mesh, PartitionSpec as P

TWO_PI = 6.283185307179586
BOX = 64.0
MIB = 1024 * 1024
SINE = (4.4428679, -7.30744342, 3.59478803, -0.7843739)
COSINE = (1.41420408, -6.97764207, 5.71523842, -1.72834863)
OVER = ("xh", "z")
ACROSS = ("xl", "y")
SWAP = [(0, 1), (1, 0)]
DEPTH = 16
SHARED = 4
TILE = 512
WHOLE = pl.BlockSpec(memory_space=pltpu.VMEM)
SCALAR = pl.BlockSpec(memory_space=pltpu.SMEM)
FAR = pl.BlockSpec(memory_space=pltpu.HBM)


def triple(x):
    hi = x.astype(jnp.bfloat16)
    rest = x - hi.astype(jnp.float32)
    mid = rest.astype(jnp.bfloat16)
    low = (rest - mid.astype(jnp.float32)).astype(jnp.bfloat16)
    return [hi, mid, low]


def places(frac):
    n = frac.shape[1]
    rest = DEPTH - 10
    return jnp.concatenate(
        triple(frac) + [jnp.ones((1, n), jnp.bfloat16), jnp.zeros((rest, n), jnp.bfloat16)], axis=0
    )


def contract(left, right, dims):
    return lax.dot_general(left, right, (dims, ((), ())), preferred_element_type=jnp.float32)


def cos_sin(turns):
    r = turns - jnp.round(turns)
    t = r * r
    s = (((SINE[3] * t + SINE[2]) * t + SINE[1]) * t + SINE[0]) * r
    c = ((COSINE[3] * t + COSINE[2]) * t + COSINE[1]) * t + COSINE[0]
    return (1.0 - s * s).astype(jnp.bfloat16), (s * c).astype(jnp.bfloat16)


def params(mib):
    return pltpu.CompilerParams(vmem_limit_bytes=mib * MIB)


def cost(flops, moved):
    return pl.CostEstimate(flops=flops, bytes_accessed=moved, transcendentals=0)


def steps_of(miller, core):
    kn = miller.shape[1]
    mills = miller.astype(jnp.float32) * (1.0 - 2.0 * core)
    rows = [mills, mills, mills, jnp.full((1, kn), 0.25 * core), jnp.zeros((DEPTH - 10, kn), jnp.float32)]
    return jnp.concatenate(rows, axis=0).astype(jnp.bfloat16)


def prepare_kernel(scale, miller, filter_weight, weights, columns):
    kn = miller.shape[1]
    column = jnp.concatenate([miller[...].astype(jnp.float32), jnp.zeros((5, kn), jnp.float32)], axis=0).T
    columns[...] = column
    length = jnp.sqrt(jnp.sum(column * column, axis=1, keepdims=True))
    count = filter_weight.shape[0]
    centres = lax.broadcasted_iota(jnp.int32, (1, count), 1).astype(jnp.float32) * (14.0 / (count - 1))
    basis = jnp.exp(-((length - centres) ** 2))
    weights[...] = scale * jnp.dot(
        basis, filter_weight[...], precision=lax.Precision.HIGHEST, preferred_element_type=jnp.float32
    )


def prepare(miller, filter_weight, scale):
    kn = miller.shape[1]
    return pl.pallas_call(
        functools.partial(prepare_kernel, scale),
        in_specs=[WHOLE, WHOLE],
        out_specs=[WHOLE] * 2,
        out_shape=[
            jax.ShapeDtypeStruct((kn, filter_weight.shape[1]), jnp.float32),
            jax.ShapeDtypeStruct((kn, 8), jnp.float32),
        ],
        compiler_params=params(4),
        cost_estimate=cost(10**6, 10**5),
        name="prepare",
    )(miller, filter_weight)


def factors_kernel(tile, core, frac, species, feats, cot, miller, gain, emb, tab, keep, give, acc, held):
    n, ch = feats.shape
    kn = miller.shape[1]
    kinds = gain.shape[0]
    acc[...] = jnp.zeros_like(acc)
    held[...] = steps_of(miller[...], core[0]).T
    gains3 = jnp.concatenate(triple(gain[...]), axis=0)

    def part(frac, species, feats, cot, emb, tab):
        place = places(frac[...])
        onehot = (lax.broadcasted_iota(jnp.int32, (kinds, tile), 0) == species[...]).astype(jnp.float32)
        onehot = onehot.astype(jnp.bfloat16)
        gains = contract(jnp.concatenate([onehot, onehot, onehot], axis=0), gains3, ((0,), (0,)))
        rows = (feats[...].astype(jnp.float32) * gains).astype(jnp.bfloat16)
        emb[...] = rows
        for at in range(0, tile, 256):
            c, s = cos_sin(contract(held[...], place[:, at:at + 256], ((1,), (0,))))
            tab[0:kn, at:at + 256] = c
            tab[kn:2 * kn, at:at + 256] = s
        both = jnp.concatenate([rows, cot[...]], axis=1)
        acc[...] += contract(tab[...], both, ((1,), (0,)))

    pltpu.emit_pipeline(
        part,
        grid=(n // tile,),
        in_specs=[
            pl.BlockSpec((3, tile), lambda i: (0, i)),
            pl.BlockSpec((1, tile), lambda i: (0, i)),
            pl.BlockSpec((tile, ch), lambda i: (i, 0)),
            pl.BlockSpec((tile, ch), lambda i: (i, 0)),
        ],
        out_specs=[
            pl.BlockSpec((tile, ch), lambda i: (i, 0)),
            pl.BlockSpec((2 * kn, tile), lambda i: (0, i)),
        ],
    )(frac, species, feats, cot, emb, tab)
    keep[...] = acc[0:kn, :].astype(jnp.bfloat16)
    give[...] = acc[kn:2 * kn, :].astype(jnp.bfloat16)


def factors(core, frac, species, feats, cot, miller, gain, tile=1024):
    n, ch = feats.shape
    kn = miller.shape[1]
    return pl.pallas_call(
        functools.partial(factors_kernel, tile),
        in_specs=[SCALAR, FAR, FAR, FAR, FAR, WHOLE, WHOLE],
        out_specs=[FAR, FAR, WHOLE, WHOLE],
        out_shape=[
            jax.ShapeDtypeStruct((n, ch), jnp.bfloat16),
            jax.ShapeDtypeStruct((2 * kn, n), jnp.bfloat16),
            jax.ShapeDtypeStruct((kn, 2 * ch), jnp.bfloat16),
            jax.ShapeDtypeStruct((kn, 2 * ch), jnp.bfloat16),
        ],
        scratch_shapes=[
            pltpu.VMEM((2 * kn, 2 * ch), jnp.float32),
            pltpu.VMEM((kn, DEPTH), jnp.bfloat16),
        ],
        compiler_params=params(58),
        cost_estimate=cost(8 * n * kn * ch, 8 * n * ch + 4 * n * kn),
        name="factors",
    )(core, frac, species, feats, cot, miller, gain)


def pair_kernel(keep, got, out):
    out[...] = (keep[...].astype(jnp.float32) + got[...].astype(jnp.float32)).astype(jnp.bfloat16)


def pair_of(keep, got):
    return pl.pallas_call(
        pair_kernel,
        in_specs=[WHOLE, WHOLE],
        out_specs=WHOLE,
        out_shape=jax.ShapeDtypeStruct(keep.shape, jnp.bfloat16),
        compiler_params=params(4),
        cost_estimate=cost(10**6, 10**4),
        name="pair",
    )(keep, got)


def panel_kernel(where, spread, weights, out):
    groups, rows, width = spread.shape
    total = spread[0].astype(jnp.float32)
    for i in range(1, groups):
        total += spread[i].astype(jnp.float32)
    w = weights[pl.ds(pl.multiple_of(where[0] * rows, rows), rows), :]
    panel = (total * jnp.concatenate([w] * (width // w.shape[1]), axis=1)).astype(jnp.bfloat16)
    for i in range(groups):
        out[i] = panel


def panel_of(where, spread, weights):
    return pl.pallas_call(
        panel_kernel,
        in_specs=[SCALAR, WHOLE, WHOLE],
        out_specs=WHOLE,
        out_shape=jax.ShapeDtypeStruct(spread.shape, jnp.bfloat16),
        compiler_params=params(4),
        cost_estimate=cost(10**6, 10**4),
        name="panel",
    )(where, spread, weights)


def copies_kernel(core, mine, miller, out):
    blocks, _, ch = out.shape
    kn = miller.shape[1]
    steps = steps_of(miller[...], core[0])
    for i in range(blocks):
        out[i, 0:kn, :] = mine[:, :ch]
        out[i, kn:kn + DEPTH, :] = steps


def copies_of(core, mine, miller, width, blocks):
    kn = miller.shape[1]
    return pl.pallas_call(
        copies_kernel,
        in_specs=[SCALAR, WHOLE, WHOLE],
        out_specs=WHOLE,
        out_shape=jax.ShapeDtypeStruct((blocks, kn + DEPTH, width), jnp.bfloat16),
        compiler_params=params(6),
        cost_estimate=cost(10**6, 10**6),
        name="copies",
    )(core, mine, miller)


def forces_kernel(scale, sign, tab, cot, emb, mine, other, columns, out, spread, rows):
    kn = columns.shape[0]
    tile = cot.shape[0]
    wide = spread.shape[2]
    steps = pl.num_programs(0)
    step = pl.program_id(0)
    each = tile // wide

    @pl.when(step == 0)
    def _():
        for d in range(3):
            spread[d] = jnp.broadcast_to(columns[:, d:d + 1], spread.shape[1:])

    factor = sign[0] * scale
    for j in range(each):
        at = j * wide
        both = jnp.concatenate([cot[at:at + wide, :], emb[at:at + wide, :]], axis=1)
        x = contract(mine[...], both, ((1,), (1,)))
        y = contract(other[...], both, ((1,), (1,)))
        c = tab[0:kn, at:at + wide].astype(jnp.float32)
        s = tab[kn:2 * kn, at:at + wide].astype(jnp.float32)
        grads = c * y - s * x
        for d in range(3):
            rows[pl.ds(d * each * steps + step * each + j, 1), :] = (
                jnp.sum(spread[d] * grads, axis=0, keepdims=True) * factor
            )

    @pl.when(step == steps - 1)
    def _():
        high = rows[...].astype(jnp.bfloat16)
        out[0:rows.shape[0], :] = high
        out[rows.shape[0]:, :] = (rows[...] - high.astype(jnp.float32)).astype(jnp.bfloat16)


def forces_of(sign, tab, cot, emb, mine, other, columns, scale, tile=1024):
    n, ch = cot.shape
    kn = columns.shape[0]
    count = 3 * n // ch
    return pl.pallas_call(
        functools.partial(forces_kernel, scale),
        grid=(n // tile,),
        in_specs=[
            SCALAR,
            pl.BlockSpec((2 * kn, tile), lambda i: (0, i)),
            pl.BlockSpec((tile, ch), lambda i: (i, 0)),
            pl.BlockSpec((tile, ch), lambda i: (i, 0)),
            pl.BlockSpec(mine.shape, lambda i: (0, 0)),
            pl.BlockSpec(other.shape, lambda i: (0, 0)),
            pl.BlockSpec(columns.shape, lambda i: (0, 0)),
        ],
        out_specs=pl.BlockSpec((2 * count, ch), lambda i: (0, 0)),
        out_shape=jax.ShapeDtypeStruct((2 * count, ch), jnp.bfloat16),
        scratch_shapes=[pltpu.VMEM((3, kn, ch), jnp.float32), pltpu.VMEM((count, ch), jnp.float32)],
        compiler_params=params(58),
        cost_estimate=cost(2000 * n * kn, 4 * n * kn + 4 * n * ch),
        name="forces",
    )(sign, tab, cot, emb, mine, other, columns)


def total_kernel(start, parts, out):
    count = (parts.shape[1] - start) // 2
    each = count // out.shape[0]
    wide = parts.shape[2]
    total = jnp.zeros((count, wide), jnp.float32)
    for b in range(parts.shape[0]):
        total += parts[b, start:start + count, :].astype(jnp.float32)
        total += parts[b, start + count:start + 2 * count, :].astype(jnp.float32)
    for d in range(out.shape[0]):
        for j in range(each):
            out[d:d + 1, j * wide:(j + 1) * wide] = total[d * each + j:d * each + j + 1, :]


def total_of(parts, start, n):
    return pl.pallas_call(
        functools.partial(total_kernel, start),
        in_specs=[WHOLE],
        out_specs=WHOLE,
        out_shape=jax.ShapeDtypeStruct((3, n), jnp.float32),
        compiler_params=params(8),
        cost_estimate=cost(10**6, 10**6),
        name="total",
    )(parts)


def rows_of(scale, frac, feats, mine, other):
    blocks = mine.shape[0]
    kn = mine.shape[1] - DEPTH
    place = places(frac[...]).T
    total = jnp.zeros(feats.shape, jnp.float32)
    for b in range(blocks):
        c, s = cos_sin(contract(place, mine[b, kn:kn + DEPTH, :], ((1,), (0,))))
        total += contract(c, mine[b, 0:kn, :], ((1,), (0,)))
        total += contract(s, other[b, 0:kn, :], ((1,), (0,)))
    return (feats[...].astype(jnp.float32) + total * scale).astype(jnp.bfloat16)


def share_kernel(scale, where, force, frac, feats, mine, other, out):
    rows = rows_of(scale, frac, feats, mine, other)
    share = rows.shape[0]
    for b in range(out.shape[0]):
        out[b, 0:share, :] = rows
        out[b, share:, :] = force[...]


def rest_kernel(scale, frac, feats, mine, other, out):
    out[...] = rows_of(scale, frac, feats, mine, other)


def share_of(where, force, frac, feats, mine, other, scale, share):
    n, ch = feats.shape
    blocks = mine.shape[0]
    long = share + force.shape[0]
    return pl.pallas_call(
        functools.partial(share_kernel, scale),
        grid_spec=pltpu.PrefetchScalarGridSpec(
            num_scalar_prefetch=1,
            grid=(1,),
            in_specs=[
                pl.BlockSpec(force.shape, lambda i, at: (0, 0)),
                pl.BlockSpec((3, share), lambda i, at: (0, at[0])),
                pl.BlockSpec((share, ch), lambda i, at: (at[0], 0)),
                pl.BlockSpec(mine.shape, lambda i, at: (0, 0, 0)),
                pl.BlockSpec(other.shape, lambda i, at: (0, 0, 0)),
            ],
            out_specs=pl.BlockSpec((blocks, long, ch), lambda i, at: (0, 0, 0)),
        ),
        out_shape=jax.ShapeDtypeStruct((blocks, long, ch), jnp.bfloat16),
        compiler_params=params(58),
        cost_estimate=cost(10**9, 10**6),
        name="share",
    )(where, force, frac, feats, mine, other)


def rest_of(frac, feats, mine, other, scale, start, tile):
    n, ch = feats.shape
    first = start // tile
    return pl.pallas_call(
        functools.partial(rest_kernel, scale),
        grid=((n - start) // tile,),
        in_specs=[
            pl.BlockSpec((3, tile), lambda i: (0, first + i)),
            pl.BlockSpec((tile, ch), lambda i: (first + i, 0)),
            pl.BlockSpec(mine.shape, lambda i: (0, 0, 0)),
            pl.BlockSpec(other.shape, lambda i: (0, 0, 0)),
        ],
        out_specs=pl.BlockSpec((tile, ch), lambda i: (first + i, 0)),
        out_shape=jax.ShapeDtypeStruct((n, ch), jnp.bfloat16),
        compiler_params=params(58),
        cost_estimate=cost(10**10, 10**6),
        name="rest",
    )(frac, feats, mine, other)


def across(x, axes):
    return lax.all_to_all(x, axes, 0, 0)


def body(frac, species, feats, cot, miller, gain, filter_weight):
    n, ch = feats.shape
    kn = miller.shape[1]
    inv_n = 1.0 / math.sqrt(n * lax.axis_size(("xh", "z", "core")))
    inv_k = 1.0 / math.sqrt(kn * lax.axis_size(ACROSS))
    groups = lax.axis_size(OVER)
    blocks = lax.axis_size(ACROSS)
    rows = kn // groups
    core = jnp.full((1,), lax.axis_index("core").astype(jnp.float32))
    over = jnp.full((1,), lax.axis_index(OVER), jnp.int32)
    spot = jnp.full((1,), lax.axis_index(ACROSS), jnp.int32)

    emb, tab, keep, give = factors(core, frac, species.reshape(1, n), feats, cot, miller, gain)
    pair = pair_of(keep, lax.ppermute(give, "core", SWAP))
    pair, miller = lax.optimization_barrier((pair, miller))
    spread = across(pair.reshape(groups, rows, 2 * ch), OVER)
    weights, columns = prepare(miller, filter_weight, inv_n)
    spread, weights = lax.optimization_barrier((spread, weights))
    mine = across(panel_of(over, spread, weights), OVER).reshape(kn, 2 * ch)

    far = across(copies_of(core, mine, miller, ch, blocks), ACROSS)
    other = lax.ppermute(mine, "core", SWAP)
    force = forces_of(1.0 - 2.0 * core, tab, cot, emb, mine, other, columns, -TWO_PI / BOX * inv_k)
    far, force = lax.optimization_barrier((far, force))
    swapped = lax.ppermute(far, "core", SWAP)
    share = n // blocks * SHARED // 8
    part = share_of(spot, force, frac, feats, far, swapped, inv_k, share)
    part, frac = lax.optimization_barrier((part, frac))
    gathered = across(part, ACROSS)
    rest = rest_of(frac, feats, far, swapped, inv_k, share * blocks, TILE)
    gathered, rest = lax.optimization_barrier((gathered, rest))
    updated = lax.dynamic_update_slice(rest, gathered[:, :share].reshape(share * blocks, ch), (0, 0))
    return updated, total_of(gathered, share, n)


def solution(mesh):
    sizes = dict(mesh.shape)
    fine = Mesh(mesh.devices.reshape(2, sizes["dom"] // 4, 2, 2, sizes["ka"] // 2), ("xh", "z", "core", "xl", "y"))
    dom = ("xh", "z", "core")
    placed = (P(None, dom), P(dom), P(dom, None), P(dom, None), P(None, ACROSS), P(), P())
    return jax.shard_map(
        body,
        mesh=fine,
        in_specs=placed,
        out_specs=(P(dom, None), P(None, dom)),
        check_vma=False,
    )
```

time: 438 us -> 108 us (0.25)
  waiting for transfers between devices: 340 us -> 14.7 us
  Pallas kernels: 0 us -> 43.7 us
  matrix products: 43.4 us -> 0 us
  starting transfers between devices: 0.26 us -> 27.8 us
  blocking collectives: 31.7 us -> 14.6 us
  between operations: 14.2 us -> 0.75 us
  other arithmetic: 4.77 us -> 0 us
    psum x2 -> x0, waiting for transfers between devices: 340 us -> none  [the longest x1 272 us: body(): sr, si, gr, gi = lax.psum((terms[0], terms[1], terms[2], terms[3]), 'dom')]
    pallas_call x0 -> x9, Pallas kernels: none -> 43.7 us  [the longest x1 18.5 us: rest_of(): pl.pallas_call(functools.partial(rest_kernel, scale), grid=((n - start) /...]
    dot_general x14 -> x0, matrix products: 43.4 us -> none  [the longest x1 20.3 us: phase_tables(): lax.dot_general(frac, miller.astype(jnp.float32), (((0,), (0,)), ((), ())...]
    psum x1 -> x0, blocking collectives: 31.7 us -> none  [body(): total, forces = lax.psum((message_part, force_part), 'ka')]
    all_to_all x0 -> x3, starting transfers between devices: none -> 16.8 us  [across(): return lax.all_to_all(x, axes, 0, 0)]
    all_to_all x0 -> x1, blocking collectives: none -> 14.6 us  [across(): return lax.all_to_all(x, axes, 0, 0)]
    ppermute x0 -> x3, starting transfers between devices: none -> 11 us  [the longest x1 4.36 us: body(): swapped = lax.ppermute(far, 'core', SWAP)]
    all_to_all x0 -> x3, waiting for transfers between devices: none -> 9.83 us  [across(): return lax.all_to_all(x, axes, 0, 0)]
  transfers between devices with their start and end apart: 2 -> 6, of which waited for: 2 -> 5; matrix products, arithmetic and copies ran while one was open for 2% -> 0% of each run, Pallas kernels for 0% -> 24%
where the time goes in v2:
time: 108 us; the launch traced here: 107 us
  Pallas kernels  43.7 us (40%)
  starting transfers between devices  27.8 us (26%)
  waiting for transfers between devices  14.7 us (14%)
  blocking collectives  14.6 us (14%)
  local copies, waits for them, and re-layouts  4.97 us (5%)
    pallas_call x1, Pallas kernels, rest_of(): pl.pallas_call(functools.partial(rest_kernel, scale), grid=((n - start) /...  18.5 us
    all_to_all x3, starting transfers between devices, across(): return lax.all_to_all(x, axes, 0, 0)  16.8 us
    all_to_all x1, blocking collectives, across(): return lax.all_to_all(x, axes, 0, 0)  14.6 us
    pallas_call x1, Pallas kernels, factors(): pl.pallas_call(functools.partial(factors_kernel, tile), in_specs=[SCALAR,...  10.2 us
    all_to_all x3, waiting for transfers between devices, across(): return lax.all_to_all(x, axes, 0, 0)  9.83 us
    pallas_call x1, Pallas kernels, forces_of(): pl.pallas_call(functools.partial(forces_kernel, scale), grid=(n // tile,)...  6.84 us
    pallas_call x1, Pallas kernels, share_of(): pl.pallas_call(functools.partial(share_kernel, scale), grid_spec=pltpu.Pr...  5.06 us
    unnamed x20, local copies, waits for them, and re-layouts  4.84 us
  transfers between devices with their start and end apart: 6, of which 5 were waited for; matrix products, arithmetic and copies ran while one was open for 0% of the time, Pallas kernels for 24%

profile of v2, /device:TPU:1, one launch (start us, length us, event | category | flops | bytes accessed | tf_op | source)
XLA Modules:
  0.0 106.6 jit_solution(18363027934087728984)
XLA Ops:
  0.6 0.0 copy-start.3
  0.6 0.0 copy-start.4
  0.7 10.2 %factors.1 = (bf16[4096,256]{1,0:T(8,128)(2,1)}, bf16[512,4096]{1,0:T(8,128)(2,1)}, bf16[256,512]{1,0:T(8,128)(2,1)}, bf16[256,512]{1,0:T(8,128)(2,1)}) custom-call(f32[1]{0:T(128)} %bitcast.1.core, f32[3,4096]{1,0:T(4,128)} %frac.4, s32[1,4096]{1,0:T(1,128)} %bitcast.11, bf16[4096,256]{1,0:T(8,128)(2,1)} %feats.5, bf16[4096,256]{1,0:T(8,128)(2,1)} %cot.3, ...), custom_call_target="tpu_custom_call" | custom-call | flops 2147483648 | bytes 12582912 | tf_op jit(solution)/shard_map/factors/pallas_call | solution.py:142
  10.8 3.2 %collective-permute-start = (bf16[256,512]{1,0:T(8,128)(2,1)}, bf16[256,512]{1,0:T(8,128)(2,1)S(1)}, u32[]{:S(2)}, u32[]{:S(2)}) collective-permute-start(bf16[256,512]{1,0:T(8,128)(2,1)} %get-tuple-element.19), channel_id=1, source_target_pairs={{0,8},{8,0},{1,9},{9,1},{2,10},{10,2},{3,11},{11,3},{4,12},{12,4},... | collective-permute-start | bytes 786440 | tf_op jit(solution)/shard_map/ppermute | solution.py:393
  14.1 1.4 %collective-permute-done.got = bf16[256,512]{1,0:T(8,128)(2,1)S(1)} collective-permute-done((bf16[256,512]{1,0:T(8,128)(2,1)}, bf16[256,512]{1,0:T(8,128)(2,1)S(1)}, u32[]{:S(2)}, u32[]{:S(2)}) %collective-permute-start) | collective-permute-done | bytes 262176 | tf_op jit(solution)/shard_map/ppermute | solution.py:393
  15.4 0.0 copy-start.1
  15.5 0.9 copy-done.1
  16.4 0.8 pair.1
  17.2 9.0 %all-to-all-start = ((bf16[16,16,512]{2,1,0:T(8,128)(2,1)}), bf16[16,16,512]{2,1,0:T(8,128)(2,1)S(1)}, u32[]{:S(2)}, u32[]{:S(2)}) async-start(bf16[16,16,512]{2,1,0:T(8,128)(2,1)} %bitcast.4), calls=%async_computation | async-start | bytes 524288 | tf_op jit(solution)/shard_map/all_to_all | solution.py:377
  26.2 0.0 copy-done.3
  26.2 0.0 copy-done.4
  26.2 0.5 prepare.1
  26.8 0.0 copy-start.2
  26.8 0.6 copy-done.2
  27.4 9.3 %all-to-all-done.spread = bf16[16,16,512]{2,1,0:T(8,128)(2,1)S(1)} async-done(((bf16[16,16,512]{2,1,0:T(8,128)(2,1)}), bf16[16,16,512]{2,1,0:T(8,128)(2,1)S(1)}, u32[]{:S(2)}, u32[]{:S(2)}) %all-to-all-start) | async-done | bytes 262176 | tf_op jit(solution)/shard_map/all_to_all | solution.py:377
  36.7 14.6 %all_to_all.20 = bf16[16,16,512]{2,1,0:T(8,128)(2,1)S(1)} all-to-all(bf16[16,16,512]{2,1,0:T(8,128)(2,1)S(1)} %panel.1), channel_id=1, replica_groups=mesh['xh'=2,'z'=8,'core'=2,'xl'=2,'y'=4] {'xh','z'}, dimensions={0} | all-to-all | bytes 524288 | tf_op jit(solution)/shard_map/all_to_all | solution.py:377
  51.3 0.0 copy-start
  51.3 1.1 %copies.1 = bf16[8,272,256]{2,1,0:T(8,128)(2,1)} custom-call(f32[1]{0:T(128)} %bitcast.1.core, bf16[256,512]{1,0:T(8,128)(2,1)S(1)} %bitcast.7, s32[3,256]{1,0:T(4,128)S(1)} %copy-done.3), custom_call_target="tpu_custom_call" | custom-call | flops 1000000 | bytes 1000000 | tf_op jit(solution)/shard_map/copies/pallas_call | solution.py:212
  52.4 4.2 %all-to-all-start.2 = ((bf16[8,272,256]{2,1,0:T(8,128)(2,1)}), bf16[8,272,256]{2,1,0:T(8,128)(2,1)S(1)}, u32[]{:S(2)}, u32[]{:S(2)}) async-start(bf16[8,272,256]{2,1,0:T(8,128)(2,1)} %copies.1), calls=%async_computation.2 | async-start | bytes 2228224 | tf_op jit(solution)/shard_map/all_to_all | solution.py:377
  56.6 3.4 %collective-permute-start.1 = (bf16[256,512]{1,0:T(8,128)(2,1)S(1)}, bf16[256,512]{1,0:T(8,128)(2,1)S(1)}, u32[]{:S(2)}, u32[]{:S(2)}) collective-permute-start(bf16[256,512]{1,0:T(8,128)(2,1)S(1)} %bitcast.8), channel_id=1, source_target_pairs={{0,8},{8,0},{1,9},{9,1},{2,10},{10,2},{3,11},{11,3},{4,12},{12,4},... | collective-permute-start | bytes 786440 | tf_op jit(solution)/shard_map/ppermute | solution.py:401
  60.0 1.2 %collective-permute-done.1.other = bf16[256,512]{1,0:T(8,128)(2,1)S(1)} collective-permute-done((bf16[256,512]{1,0:T(8,128)(2,1)S(1)}, bf16[256,512]{1,0:T(8,128)(2,1)S(1)}, u32[]{:S(2)}, u32[]{:S(2)}) %collective-permute-start.1) | collective-permute-done | bytes 262176 | tf_op jit(solution)/shard_map/ppermute | solution.py:401
  61.2 0.0 copy-start.7
  61.2 0.0 copy-done
  61.2 0.7 copy-done.7
  61.9 6.8 %forces.1.force = bf16[96,256]{1,0:T(8,128)(2,1)} custom-call(f32[1]{0:T(128)S(6)} %sub.3.sign, bf16[512,4096]{1,0:T(8,128)(2,1)} %get-tuple-element.25.tab, bf16[4096,256]{1,0:T(8,128)(2,1)} %cot.3, bf16[4096,256]{1,0:T(8,128)(2,1)} %get-tuple-element.26.emb, bf16[256,512]{1,0:T(8,128)(2,1)} %bitcast.9, bf16[256,512]{1,0:T(8,128)(2,1)} %copy-done.7, ...), custom_call_target="tpu_custom_call" | custom-call | flops 2097152000 | bytes 8388608 | tf_op jit(solution)/shard_map/forces/pallas_call | solution.py:261
  68.7 0.0 all-to-all-done.2.mine
  68.7 0.0 copy-start.5
  68.7 4.4 %collective-permute-start.2 = (bf16[8,272,256]{2,1,0:T(8,128)(2,1)S(1)}, bf16[8,272,256]{2,1,0:T(8,128)(2,1)S(1)}, u32[]{:S(2)}, u32[]{:S(2)}) collective-permute-start(bf16[8,272,256]{2,1,0:T(8,128)(2,1)S(1)} %all-to-all-done.2.mine), channel_id=1, source_target_pairs={{0,8},{8,0},{1,9},{9,1},{2,10},{10,2},{3,11},{11,3},{4,12},{12,4},... | collective-permute-start | bytes 3342344 | tf_op jit(solution)/shard_map/ppermute | solution.py:404
  73.1 2.4 %collective-permute-done.2.other = bf16[8,272,256]{2,1,0:T(8,128)(2,1)S(1)} collective-permute-done((bf16[8,272,256]{2,1,0:T(8,128)(2,1)S(1)}, bf16[8,272,256]{2,1,0:T(8,128)(2,1)S(1)}, u32[]{:S(2)}, u32[]{:S(2)}) %collective-permute-start.2) | collective-permute-done | bytes 1114144 | tf_op jit(solution)/shard_map/ppermute | solution.py:404
  75.5 0.0 copy-start.6
  75.5 0.0 copy-done.5
  75.5 1.0 copy-done.6
  76.5 5.1 %share.1 = bf16[8,352,256]{2,1,0:T(8,128)(2,1)} custom-call(s32[1]{0:T(128)} %bitcast.where, bf16[96,256]{1,0:T(8,128)(2,1)} %forces.1.force, f32[3,4096]{1,0:T(4,128)} %frac.4, bf16[4096,256]{1,0:T(8,128)(2,1)} %feats.5, bf16[8,272,256]{2,1,0:T(8,128)(2,1)} %copy-done.5, bf16[8,272,256]{2,1,0:T(8,128)(2,1)} %copy-done.6), custom_call_target="tpu_custom_call" | custom-call | flops 1000000000 | bytes 1000000 | tf_op jit(solution)/shard_map/share/pallas_call | solution.py:335
  81.5 3.6 %all-to-all-start.3 = ((bf16[8,352,256]{2,1,0:T(8,128)(2,1)}), bf16[8,352,256]{2,1,0:T(8,128)(2,1)S(1)}, u32[]{:S(2)}, u32[]{:S(2)}) async-start(bf16[8,352,256]{2,1,0:T(8,128)(2,1)} %share.1), calls=%async_computation.3 | async-start | bytes 2883584 | tf_op jit(solution)/shard_map/all_to_all | solution.py:377
  85.1 18.5 %rest.1 = bf16[4096,256]{1,0:T(8,128)(2,1)} custom-call(f32[3,4096]{1,0:T(4,128)} %frac.4, bf16[4096,256]{1,0:T(8,128)(2,1)} %feats.5, bf16[8,272,256]{2,1,0:T(8,128)(2,1)} %copy-done.5, bf16[8,272,256]{2,1,0:T(8,128)(2,1)} %copy-done.6), custom_call_target="tpu_custom_call" | custom-call | flops 10000000000 | bytes 1000000 | tf_op jit(solution)/shard_map/rest/pallas_call | solution.py:359
  103.6 0.0 copy-start.8
  103.6 0.6 all-to-all-done.3.parts
  104.2 0.7 total.1
  104.9 0.1 slice.3
  105.0 0.2 copy-done.8
  105.2 0.1 constant_dynamic-update-slice_fusion
  105.3 0.0 copy-start.9
  105.3 1.3 %copy-done.9 = bf16[4096,256]{1,0:T(8,128)(2,1)} copy-done((bf16[4096,256]{1,0:T(8,128)(2,1)}, bf16[4096,256]{1,0:T(8,128)(2,1)S(1)}, u32[]{:S(2)}) %copy-start.9) | copy-done | bytes 2097176
  (1 shorter events, 0.0 us)
Async XLA Ops:
  0.6 25.6 %copy-start.3 = (s32[3,256]{1,0:T(4,128)S(1)}, s32[3,256]{1,0:T(4,128)}, u32[]{:S(2)}) copy-start(s32[3,256]{1,0:T(4,128)} %miller.3) | copy-start | bytes 9220
  0.6 25.6 %copy-start.4 = (f32[16,256]{1,0:T(8,128)S(1)}, f32[16,256]{1,0:T(8,128)}, u32[]{:S(2)}) copy-start(f32[16,256]{1,0:T(8,128)} %filter_weight.1) | copy-start | bytes 49156
  10.8 4.6 %collective-permute-start = (bf16[256,512]{1,0:T(8,128)(2,1)}, bf16[256,512]{1,0:T(8,128)(2,1)S(1)}, u32[]{:S(2)}, u32[]{:S(2)}) collective-permute-start(bf16[256,512]{1,0:T(8,128)(2,1)} %get-tuple-element.19), channel_id=1, source_target_pairs={{0,8},{8,0},{1,9},{9,1},{2,10},{10,2},{3,11},{11,3},{4,12},{12,4},... | collective-permute-start | bytes 786440 | tf_op jit(solution)/shard_map/ppermute | solution.py:393
  15.4 0.9 copy-start.1
  17.2 19.5 %all-to-all-start = ((bf16[16,16,512]{2,1,0:T(8,128)(2,1)}), bf16[16,16,512]{2,1,0:T(8,128)(2,1)S(1)}, u32[]{:S(2)}, u32[]{:S(2)}) async-start(bf16[16,16,512]{2,1,0:T(8,128)(2,1)} %bitcast.4), calls=%async_computation | async-start | bytes 524288 | tf_op jit(solution)/shard_map/all_to_all | solution.py:377
  26.8 0.7 copy-start.2
  51.3 9.9 %copy-start = (bf16[16,16,512]{2,1,0:T(8,128)(2,1)}, bf16[16,16,512]{2,1,0:T(8,128)(2,1)S(1)}, u32[]{:S(2)}) copy-start(bf16[16,16,512]{2,1,0:T(8,128)(2,1)S(1)} %all_to_all.20) | copy-start | bytes 786436
  52.4 16.3 %all-to-all-start.2 = ((bf16[8,272,256]{2,1,0:T(8,128)(2,1)}), bf16[8,272,256]{2,1,0:T(8,128)(2,1)S(1)}, u32[]{:S(2)}, u32[]{:S(2)}) async-start(bf16[8,272,256]{2,1,0:T(8,128)(2,1)} %copies.1), calls=%async_computation.2 | async-start | bytes 2228224 | tf_op jit(solution)/shard_map/all_to_all | solution.py:377
  56.6 4.6 %collective-permute-start.1 = (bf16[256,512]{1,0:T(8,128)(2,1)S(1)}, bf16[256,512]{1,0:T(8,128)(2,1)S(1)}, u32[]{:S(2)}, u32[]{:S(2)}) collective-permute-start(bf16[256,512]{1,0:T(8,128)(2,1)S(1)} %bitcast.8), channel_id=1, source_target_pairs={{0,8},{8,0},{1,9},{9,1},{2,10},{10,2},{3,11},{11,3},{4,12},{12,4},... | collective-permute-start | bytes 786440 | tf_op jit(solution)/shard_map/ppermute | solution.py:401
  61.2 0.7 copy-start.7
  68.7 6.8 %copy-start.5 = (bf16[8,272,256]{2,1,0:T(8,128)(2,1)}, bf16[8,272,256]{2,1,0:T(8,128)(2,1)S(1)}, u32[]{:S(2)}) copy-start(bf16[8,272,256]{2,1,0:T(8,128)(2,1)S(1)} %all-to-all-done.2.mine) | copy-start | bytes 3342340
  68.7 6.7 %collective-permute-start.2 = (bf16[8,272,256]{2,1,0:T(8,128)(2,1)S(1)}, bf16[8,272,256]{2,1,0:T(8,128)(2,1)S(1)}, u32[]{:S(2)}, u32[]{:S(2)}) collective-permute-start(bf16[8,272,256]{2,1,0:T(8,128)(2,1)S(1)} %all-to-all-done.2.mine), channel_id=1, source_target_pairs={{0,8},{8,0},{1,9},{9,1},{2,10},{10,2},{3,11},{11,3},{4,12},{12,4},... | collective-permute-start | bytes 3342344 | tf_op jit(solution)/shard_map/ppermute | solution.py:404
  75.5 1.0 copy-start.6
  81.5 22.7 %all-to-all-start.3 = ((bf16[8,352,256]{2,1,0:T(8,128)(2,1)}), bf16[8,352,256]{2,1,0:T(8,128)(2,1)S(1)}, u32[]{:S(2)}, u32[]{:S(2)}) async-start(bf16[8,352,256]{2,1,0:T(8,128)(2,1)} %share.1), calls=%async_computation.3 | async-start | bytes 2883584 | tf_op jit(solution)/shard_map/all_to_all | solution.py:377
  103.6 1.6 %copy-start.8 = (bf16[4096,256]{1,0:T(8,128)(2,1)S(1)}, bf16[4096,256]{1,0:T(8,128)(2,1)}, u32[]{:S(2)}) copy-start(bf16[4096,256]{1,0:T(8,128)(2,1)} %rest.1) | copy-start | bytes 6291460
  105.3 1.3 %copy-start.9 = (bf16[4096,256]{1,0:T(8,128)(2,1)}, bf16[4096,256]{1,0:T(8,128)(2,1)S(1)}, u32[]{:S(2)}) copy-start(bf16[4096,256]{1,0:T(8,128)(2,1)S(1)} %constant_dynamic-update-slice_fusion) | copy-start | bytes 6291460

commit v3 on v2

v3 whole, which is shorter than its diff:
```python
import functools
import math

import jax
import jax.numpy as jnp
from jax import lax
from jax.experimental import pallas as pl
from jax.experimental.pallas import tpu as pltpu
from jax.sharding import Mesh, PartitionSpec as P

TWO_PI = 6.283185307179586
BOX = 64.0
MIB = 1024 * 1024
SINE = (4.4428679, -7.30744342, 3.59478803, -0.7843739)
OVER = ("xh", "z")
ACROSS = ("xl", "y")
SWAP = [(0, 1), (1, 0)]
DEPTH = 16
SHARED = 4
TILE = 1024
WHOLE = pl.BlockSpec(memory_space=pltpu.VMEM)
SCALAR = pl.BlockSpec(memory_space=pltpu.SMEM)
FAR = pl.BlockSpec(memory_space=pltpu.HBM)


def triple(x):
    hi = x.astype(jnp.bfloat16)
    rest = x - hi.astype(jnp.float32)
    mid = rest.astype(jnp.bfloat16)
    low = (rest - mid.astype(jnp.float32)).astype(jnp.bfloat16)
    return [hi, mid, low]


def places(frac):
    n = frac.shape[1]
    rest = DEPTH - 10
    return jnp.concatenate(
        triple(frac) + [jnp.ones((1, n), jnp.bfloat16), jnp.zeros((rest, n), jnp.bfloat16)], axis=0
    )


def contract(left, right, dims):
    return lax.dot_general(left, right, (dims, ((), ())), preferred_element_type=jnp.float32)


def cos_sin(turns):
    r = turns - jnp.round(turns)
    t = r * r
    s = (((SINE[3] * t + SINE[2]) * t + SINE[1]) * t + SINE[0]) * r
    square = s * s
    rest = 2.000004 - square
    return (1.0 - square).astype(jnp.bfloat16), (s * (rest * lax.rsqrt(rest))).astype(jnp.bfloat16)


def params(mib):
    return pltpu.CompilerParams(vmem_limit_bytes=mib * MIB)


def cost(flops, moved):
    return pl.CostEstimate(flops=flops, bytes_accessed=moved, transcendentals=0)


def steps_of(miller, core):
    kn = miller.shape[1]
    mills = miller.astype(jnp.float32) * (1.0 - 2.0 * core)
    rows = [mills, mills, mills, jnp.full((1, kn), 0.25 * core), jnp.zeros((DEPTH - 10, kn), jnp.float32)]
    return jnp.concatenate(rows, axis=0).astype(jnp.bfloat16)


def prepare_kernel(scale, miller, filter_weight, weights, columns):
    kn = miller.shape[1]
    column = jnp.concatenate([miller[...].astype(jnp.float32), jnp.zeros((5, kn), jnp.float32)], axis=0).T
    columns[...] = column
    length = jnp.sqrt(jnp.sum(column * column, axis=1, keepdims=True))
    count = filter_weight.shape[0]
    centres = lax.broadcasted_iota(jnp.int32, (1, count), 1).astype(jnp.float32) * (14.0 / (count - 1))
    basis = jnp.exp(-((length - centres) ** 2))
    weights[...] = scale * jnp.dot(
        basis, filter_weight[...], precision=lax.Precision.HIGHEST, preferred_element_type=jnp.float32
    )


def prepare(miller, filter_weight, scale):
    kn = miller.shape[1]
    return pl.pallas_call(
        functools.partial(prepare_kernel, scale),
        in_specs=[WHOLE, WHOLE],
        out_specs=[WHOLE] * 2,
        out_shape=[
            jax.ShapeDtypeStruct((kn, filter_weight.shape[1]), jnp.float32),
            jax.ShapeDtypeStruct((kn, 8), jnp.float32),
        ],
        compiler_params=params(4),
        cost_estimate=cost(10**6, 10**5),
        name="prepare",
    )(miller, filter_weight)


def embed(feats, species, gains3):
    kinds = gains3.shape[0] // 3
    onehot = (lax.broadcasted_iota(jnp.int32, (kinds, species.shape[1]), 0) == species).astype(jnp.float32)
    onehot = onehot.astype(jnp.bfloat16)
    gains = contract(jnp.concatenate([onehot, onehot, onehot], axis=0), gains3, ((0,), (0,)))
    return (feats.astype(jnp.float32) * gains).astype(jnp.bfloat16)


def factors_kernel(core, frac, species, feats, cot, miller, gain, keep, give, acc, held, tab):
    step = pl.program_id(0)
    kn = miller.shape[1]
    tile = frac.shape[1]

    @pl.when(step == 0)
    def _():
        acc[...] = jnp.zeros_like(acc)
        held[...] = steps_of(miller[...], core[0]).T

    place = places(frac[...])
    rows = embed(feats[...], species[...], jnp.concatenate(triple(gain[...]), axis=0))
    for at in range(0, tile, 256):
        c, s = cos_sin(contract(held[...], place[:, at:at + 256], ((1,), (0,))))
        tab[0:kn, at:at + 256] = c
        tab[kn:2 * kn, at:at + 256] = s
    both = jnp.concatenate([rows, cot[...]], axis=1)
    acc[...] += contract(tab[...], both, ((1,), (0,)))

    @pl.when(step == pl.num_programs(0) - 1)
    def _():
        keep[...] = acc[0:kn, :].astype(jnp.bfloat16)
        give[...] = acc[kn:2 * kn, :].astype(jnp.bfloat16)


def factors(core, frac, species, feats, cot, miller, gain, tile=1024):
    n, ch = feats.shape
    kn = miller.shape[1]
    return pl.pallas_call(
        factors_kernel,
        grid=(n // tile,),
        in_specs=[
            SCALAR,
            pl.BlockSpec((3, tile), lambda i: (0, i)),
            pl.BlockSpec((1, tile), lambda i: (0, i)),
            pl.BlockSpec((tile, ch), lambda i: (i, 0)),
            pl.BlockSpec((tile, ch), lambda i: (i, 0)),
            pl.BlockSpec(miller.shape, lambda i: (0, 0)),
            pl.BlockSpec(gain.shape, lambda i: (0, 0)),
        ],
        out_specs=[pl.BlockSpec((kn, 2 * ch), lambda i: (0, 0))] * 2,
        out_shape=[jax.ShapeDtypeStruct((kn, 2 * ch), jnp.bfloat16)] * 2,
        scratch_shapes=[
            pltpu.VMEM((2 * kn, 2 * ch), jnp.float32),
            pltpu.VMEM((kn, DEPTH), jnp.bfloat16),
            pltpu.VMEM((2 * kn, tile), jnp.bfloat16),
        ],
        compiler_params=params(58),
        cost_estimate=cost(8 * n * kn * ch, 8 * n * ch + 4 * n * kn),
        name="factors",
    )(core, frac, species, feats, cot, miller, gain)


def pair_kernel(keep, got, out):
    out[...] = (keep[...].astype(jnp.float32) + got[...].astype(jnp.float32)).astype(jnp.bfloat16)


def pair_of(keep, got):
    return pl.pallas_call(
        pair_kernel,
        in_specs=[WHOLE, WHOLE],
        out_specs=WHOLE,
        out_shape=jax.ShapeDtypeStruct(keep.shape, jnp.bfloat16),
        compiler_params=params(4),
        cost_estimate=cost(10**6, 10**4),
        name="pair",
    )(keep, got)


def panel_kernel(where, spread, weights, out):
    groups, rows, width = spread.shape
    total = spread[0].astype(jnp.float32)
    for i in range(1, groups):
        total += spread[i].astype(jnp.float32)
    w = weights[pl.ds(pl.multiple_of(where[0] * rows, rows), rows), :]
    panel = (total * jnp.concatenate([w] * (width // w.shape[1]), axis=1)).astype(jnp.bfloat16)
    for i in range(groups):
        out[i] = panel


def panel_of(where, spread, weights):
    return pl.pallas_call(
        panel_kernel,
        in_specs=[SCALAR, WHOLE, WHOLE],
        out_specs=WHOLE,
        out_shape=jax.ShapeDtypeStruct(spread.shape, jnp.bfloat16),
        compiler_params=params(4),
        cost_estimate=cost(10**6, 10**4),
        name="panel",
    )(where, spread, weights)


def copies_kernel(core, mine, miller, out):
    blocks, _, ch = out.shape
    kn = miller.shape[1]
    steps = steps_of(miller[...], core[0])
    for i in range(blocks):
        out[i, 0:kn, :] = mine[:, :ch]
        out[i, kn:kn + DEPTH, :] = steps


def copies_of(core, mine, miller, width, blocks):
    kn = miller.shape[1]
    return pl.pallas_call(
        copies_kernel,
        in_specs=[SCALAR, WHOLE, WHOLE],
        out_specs=WHOLE,
        out_shape=jax.ShapeDtypeStruct((blocks, kn + DEPTH, width), jnp.bfloat16),
        compiler_params=params(6),
        cost_estimate=cost(10**6, 10**6),
        name="copies",
    )(core, mine, miller)


def forces_kernel(scale, core, frac, species, feats, cot, miller, gain, mine, other, columns, out, held, spread, rows):
    kn = columns.shape[0]
    tile = cot.shape[0]
    wide = spread.shape[2]
    steps = pl.num_programs(0)
    step = pl.program_id(0)
    each = tile // wide

    @pl.when(step == 0)
    def _():
        held[...] = steps_of(miller[...], core[0]).T
        for d in range(3):
            spread[d] = jnp.broadcast_to(columns[:, d:d + 1], spread.shape[1:])

    factor = (1.0 - 2.0 * core[0]) * scale
    place = places(frac[...])
    emb = embed(feats[...], species[...], jnp.concatenate(triple(gain[...]), axis=0))
    for j in range(each):
        at = j * wide
        both = jnp.concatenate([cot[at:at + wide, :], emb[at:at + wide, :]], axis=1)
        x = contract(mine[...], both, ((1,), (1,)))
        y = contract(other[...], both, ((1,), (1,)))
        c, s = cos_sin(contract(held[...], place[:, at:at + wide], ((1,), (0,))))
        grads = c.astype(jnp.float32) * y - s.astype(jnp.float32) * x
        for d in range(3):
            rows[pl.ds(d * each * steps + step * each + j, 1), :] = (
                jnp.sum(spread[d] * grads, axis=0, keepdims=True) * factor
            )

    @pl.when(step == steps - 1)
    def _():
        out[...] = rows[...].astype(jnp.bfloat16)


def forces_of(core, frac, species, feats, cot, miller, gain, mine, other, columns, scale, tile=1024):
    n, ch = cot.shape
    kn = columns.shape[0]
    count = 3 * n // ch
    return pl.pallas_call(
        functools.partial(forces_kernel, scale),
        grid=(n // tile,),
        in_specs=[
            SCALAR,
            pl.BlockSpec((3, tile), lambda i: (0, i)),
            pl.BlockSpec((1, tile), lambda i: (0, i)),
            pl.BlockSpec((tile, ch), lambda i: (i, 0)),
            pl.BlockSpec((tile, ch), lambda i: (i, 0)),
            pl.BlockSpec(miller.shape, lambda i: (0, 0)),
            pl.BlockSpec(gain.shape, lambda i: (0, 0)),
            pl.BlockSpec(mine.shape, lambda i: (0, 0)),
            pl.BlockSpec(other.shape, lambda i: (0, 0)),
            pl.BlockSpec(columns.shape, lambda i: (0, 0)),
        ],
        out_specs=pl.BlockSpec((count, ch), lambda i: (0, 0)),
        out_shape=jax.ShapeDtypeStruct((count, ch), jnp.bfloat16),
        scratch_shapes=[
            pltpu.VMEM((kn, DEPTH), jnp.bfloat16),
            pltpu.VMEM((3, kn, ch), jnp.float32),
            pltpu.VMEM((count, ch), jnp.float32),
        ],
        compiler_params=params(58),
        cost_estimate=cost(2000 * n * kn, 4 * n * kn + 4 * n * ch),
        name="forces",
    )(core, frac, species, feats, cot, miller, gain, mine, other, columns)


def finish_kernel(share, parts, rest, out, forces, sems):
    blocks, long, wide = parts.shape
    copies = [
        pltpu.make_async_copy(parts.at[b, pl.ds(0, share), :], out.at[pl.ds(b * share, share), :], sems.at[b])
        for b in range(blocks)
    ]
    for copy in copies:
        copy.start()
    count = long - share
    each = count // forces.shape[0]
    total = jnp.zeros((count, wide), jnp.float32)
    for b in range(blocks):
        total += parts[b, share:share + count, :].astype(jnp.float32)
    for d in range(forces.shape[0]):
        for j in range(each):
            forces[d:d + 1, j * wide:(j + 1) * wide] = total[d * each + j:d * each + j + 1, :]
    for copy in copies:
        copy.wait()


def finish(parts, rest, share):
    n, ch = rest.shape
    return pl.pallas_call(
        functools.partial(finish_kernel, share),
        in_specs=[WHOLE, FAR],
        out_specs=[FAR, WHOLE],
        out_shape=[jax.ShapeDtypeStruct((n, ch), jnp.bfloat16), jax.ShapeDtypeStruct((3, n), jnp.float32)],
        scratch_shapes=[pltpu.SemaphoreType.DMA((parts.shape[0],))],
        input_output_aliases={1: 0},
        compiler_params=params(8),
        cost_estimate=cost(10**6, 10**6),
        name="finish",
    )(parts, rest)


def half_kernel(frac, mine, total, table):
    kn = mine.shape[1] - DEPTH
    place = places(frac[...]).T
    sums = jnp.zeros(total.shape, jnp.float32)
    for b in range(mine.shape[0]):
        c, s = cos_sin(contract(place, mine[b, kn:kn + DEPTH, :], ((1,), (0,))))
        sums += contract(c, mine[b, 0:kn, :], ((1,), (0,)))
        table[:, b * kn:(b + 1) * kn] = s
    total[...] = sums


def half_of(frac, mine):
    n = frac.shape[1]
    blocks, long, ch = mine.shape
    return pl.pallas_call(
        half_kernel,
        in_specs=[WHOLE, WHOLE],
        out_specs=[WHOLE, WHOLE],
        out_shape=[
            jax.ShapeDtypeStruct((n, ch), jnp.float32),
            jax.ShapeDtypeStruct((n, blocks * (long - DEPTH)), jnp.bfloat16),
        ],
        compiler_params=params(8),
        cost_estimate=cost(2 * 10**9, 10**6),
        name="half",
    )(frac, mine)


def share_kernel(scale, total, table, other, feats, force, out):
    kn = other.shape[1] - DEPTH
    share = feats.shape[0]
    sums = total[...]
    for b in range(other.shape[0]):
        sums += contract(table[:, b * kn:(b + 1) * kn], other[b, 0:kn, :], ((1,), (0,)))
    rows = (feats[...].astype(jnp.float32) + sums * scale).astype(jnp.bfloat16)
    for b in range(out.shape[0]):
        out[b, 0:share, :] = rows
        out[b, share:, :] = force[...]


def share_of(total, table, other, feats, force, scale):
    share, ch = feats.shape
    return pl.pallas_call(
        functools.partial(share_kernel, scale),
        in_specs=[WHOLE] * 5,
        out_specs=WHOLE,
        out_shape=jax.ShapeDtypeStruct((other.shape[0], share + force.shape[0], ch), jnp.bfloat16),
        compiler_params=params(8),
        cost_estimate=cost(10**9, 10**6),
        name="share",
    )(total, table, other, feats, force)


def rest_kernel(scale, frac, feats, mine, other, out):
    blocks = mine.shape[0]
    kn = mine.shape[1] - DEPTH
    place = places(frac[...]).T
    for at in range(0, feats.shape[0], 256):
        here = slice(at, at + 256)
        total = jnp.zeros((256, feats.shape[1]), jnp.float32)
        for b in range(blocks):
            c, s = cos_sin(contract(place[here], mine[b, kn:kn + DEPTH, :], ((1,), (0,))))
            total += contract(c, mine[b, 0:kn, :], ((1,), (0,)))
            total += contract(s, other[b, 0:kn, :], ((1,), (0,)))
        out[here, :] = (feats[here, :].astype(jnp.float32) + total * scale).astype(jnp.bfloat16)


def rest_of(frac, feats, mine, other, scale, start, tile):
    n, ch = feats.shape
    first = start // tile
    return pl.pallas_call(
        functools.partial(rest_kernel, scale),
        grid=((n - start) // tile,),
        in_specs=[
            pl.BlockSpec((3, tile), lambda i: (0, first + i)),
            pl.BlockSpec((tile, ch), lambda i: (first + i, 0)),
            pl.BlockSpec(mine.shape, lambda i: (0, 0, 0)),
            pl.BlockSpec(other.shape, lambda i: (0, 0, 0)),
        ],
        out_specs=pl.BlockSpec((tile, ch), lambda i: (first + i, 0)),
        out_shape=jax.ShapeDtypeStruct((n, ch), jnp.bfloat16),
        compiler_params=params(58),
        cost_estimate=cost(10**10, 10**6),
        name="rest",
    )(frac, feats, mine, other)


def across(x, axes):
    return lax.all_to_all(x, axes, 0, 0)


def body(frac, species, feats, cot, miller, gain, filter_weight):
    n, ch = feats.shape
    kn = miller.shape[1]
    inv_n = 1.0 / math.sqrt(n * lax.axis_size(("xh", "z", "core")))
    inv_k = 1.0 / math.sqrt(kn * lax.axis_size(ACROSS))
    groups = lax.axis_size(OVER)
    blocks = lax.axis_size(ACROSS)
    rows = kn // groups
    core = jnp.full((1,), lax.axis_index("core").astype(jnp.float32))
    over = jnp.full((1,), lax.axis_index(OVER), jnp.int32)
    spot = jnp.full((1,), lax.axis_index(ACROSS), jnp.int32)

    kinds = species.reshape(1, n)
    keep, give = factors(core, frac, kinds, feats, cot, miller, gain)
    pair = pair_of(keep, lax.ppermute(give, "core", SWAP))
    share = n // blocks * SHARED // 8
    pair, miller, some_frac, some_feats = lax.optimization_barrier((pair, miller, frac, feats))
    spread = across(pair.reshape(groups, rows, 2 * ch), OVER)
    weights, columns = prepare(miller, filter_weight, inv_n)
    some_frac = lax.dynamic_slice_in_dim(some_frac, spot[0] * share, share, axis=1)
    some_feats = lax.dynamic_slice_in_dim(some_feats, spot[0] * share, share, axis=0)
    spread, weights, some_frac, some_feats = lax.optimization_barrier((spread, weights, some_frac, some_feats))
    mine = across(panel_of(over, spread, weights), OVER).reshape(kn, 2 * ch)

    far = across(copies_of(core, mine, miller, ch, blocks), ACROSS)
    other = lax.ppermute(mine, "core", SWAP)
    scale = -TWO_PI / BOX * inv_k
    force = forces_of(core, frac, kinds, feats, cot, miller, gain, mine, other, columns, scale)
    far, force = lax.optimization_barrier((far, force))
    swapped = lax.ppermute(far, "core", SWAP)
    total, table = half_of(some_frac, far)
    part = share_of(total, table, swapped, some_feats, force, inv_k)
    part, frac = lax.optimization_barrier((part, frac))
    gathered = across(part, ACROSS)
    rest = rest_of(frac, feats, far, swapped, inv_k, share * blocks, TILE)
    gathered, rest = lax.optimization_barrier((gathered, rest))
    return tuple(finish(gathered, rest, share))


def solution(mesh):
    sizes = dict(mesh.shape)
    fine = Mesh(mesh.devices.reshape(2, sizes["dom"] // 4, 2, 2, sizes["ka"] // 2), ("xh", "z", "core", "xl", "y"))
    dom = ("xh", "z", "core")
    placed = (P(None, dom), P(dom), P(dom, None), P(dom, None), P(None, ACROSS), P(), P())
    return jax.shard_map(
        body,
        mesh=fine,
        in_specs=placed,
        out_specs=(P(dom, None), P(None, dom)),
        check_vma=False,
    )
```

time: 108 us -> 97.2 us (0.900)
  Pallas kernels: 43.7 us -> 39.3 us
  waiting for transfers between devices: 14.7 us -> 12.2 us
  starting transfers between devices: 27.8 us -> 25.8 us
    pallas_call x3 -> x4, Pallas kernels: 15.9 us -> 12.1 us  [the longest x1 7.32 us: factors(): pl.pallas_call(factors_kernel, grid=(n // tile,), in_specs=[SCALAR, pl.Bl...]
    pallas_call x1, Pallas kernels: 18.5 us -> 15.8 us  [rest_of(): pl.pallas_call(functools.partial(rest_kernel, scale), grid=((n - start) /...]
    unnamed x20 -> x18, local copies, waits for them, and re-layouts: 4.84 us -> 2.31 us
    ppermute x1, starting transfers between devices: 4.36 us -> 2.15 us  [body(): swapped = lax.ppermute(far, 'core', SWAP)]
    pallas_call x1, Pallas kernels: 6.84 us -> 9.04 us  [forces_of(): pl.pallas_call(functools.partial(forces_kernel, scale), grid=(n // tile,)...]
    ppermute x1, waiting for transfers between devices: 2.38 us -> 0.75 us  [body(): swapped = lax.ppermute(far, 'core', SWAP)]
    dynamic_slice x0 -> x2, local copies, waits for them, and re-layouts: none -> 1.6 us  [the longest x1 0.91 us: body(): lax.dynamic_slice_in_dim(some_feats, spot[0] * share, share, axis=0)]
  transfers between devices with their start and end apart: 6 -> 6, of which waited for: 5 -> 5; matrix products, arithmetic and copies ran while one was open for 0% -> 2% of each run, Pallas kernels for 24% -> 28%
where the time goes in v3:
time: 97.2 us; the launch traced here: 96.7 us
  Pallas kernels  39.3 us (40%)
  starting transfers between devices  25.8 us (27%)
  blocking collectives  14.6 us (15%)
  waiting for transfers between devices  12.2 us (13%)
  local copies, waits for them, and re-layouts  3.91 us (4%)
    all_to_all x3, starting transfers between devices, across(): return lax.all_to_all(x, axes, 0, 0)  17 us
    pallas_call x1, Pallas kernels, rest_of(): pl.pallas_call(functools.partial(rest_kernel, scale), grid=((n - start) /...  15.8 us
    all_to_all x1, blocking collectives, across(): return lax.all_to_all(x, axes, 0, 0)  14.6 us
    pallas_call x1, Pallas kernels, forces_of(): pl.pallas_call(functools.partial(forces_kernel, scale), grid=(n // tile,)...  9.04 us
    all_to_all x3, waiting for transfers between devices, across(): return lax.all_to_all(x, axes, 0, 0)  8.9 us
    pallas_call x1, Pallas kernels, factors(): pl.pallas_call(factors_kernel, grid=(n // tile,), in_specs=[SCALAR, pl.Bl...  7.32 us
    ppermute x1, starting transfers between devices, body(): other = lax.ppermute(mine, 'core', SWAP)  3.4 us
    ppermute x1, starting transfers between devices, body(): pair = pair_of(keep, lax.ppermute(give, 'core', SWAP))  3.24 us
  transfers between devices with their start and end apart: 6, of which 5 were waited for; matrix products, arithmetic and copies ran while one was open for 2% of the time, Pallas kernels for 28%

profile of v3, /device:TPU:1, one launch (start us, length us, event | category | flops | bytes accessed | tf_op | source)
XLA Modules:
  0.0 96.7 jit_solution(11118100324703133963)
XLA Ops:
  0.6 0.0 copy-start.5
  0.6 0.0 copy-start.6
  0.7 7.3 %factors.1 = (bf16[256,512]{1,0:T(8,128)(2,1)}, bf16[256,512]{1,0:T(8,128)(2,1)}) custom-call(f32[1]{0:T(128)} %bitcast.core, f32[3,4096]{1,0:T(4,128)} %frac.4, s32[1,4096]{1,0:T(1,128)} %bitcast.8, bf16[4096,256]{1,0:T(8,128)(2,1)} %feats.5, bf16[4096,256]{1,0:T(8,128)(2,1)} %cot.3, s32[3,256]{1,0:T(4,128)} %miller.4, f32[8,256]{1,0:T(8,128)} %gain.3), custom_call_target="tpu_custom_call" | custom-call | flops 2147483648 | bytes 12582912 | tf_op jit(solution)/shard_map/factors/pallas_call | solution.py:135
  8.0 3.2 %collective-permute-start = (bf16[256,512]{1,0:T(8,128)(2,1)}, bf16[256,512]{1,0:T(8,128)(2,1)S(1)}, u32[]{:S(2)}, u32[]{:S(2)}) collective-permute-start(bf16[256,512]{1,0:T(8,128)(2,1)} %get-tuple-element.23), channel_id=1, source_target_pairs={{0,8},{8,0},{1,9},{9,1},{2,10},{10,2},{3,11},{11,3},{4,12},{12,4},... | collective-permute-start | bytes 786440 | tf_op jit(solution)/shard_map/ppermute | solution.py:427
  11.2 1.4 %collective-permute-done.got = bf16[256,512]{1,0:T(8,128)(2,1)S(1)} collective-permute-done((bf16[256,512]{1,0:T(8,128)(2,1)}, bf16[256,512]{1,0:T(8,128)(2,1)S(1)}, u32[]{:S(2)}, u32[]{:S(2)}) %collective-permute-start) | collective-permute-done | bytes 262176 | tf_op jit(solution)/shard_map/ppermute | solution.py:427
  12.6 0.0 copy-start.3
  12.6 0.9 copy-done.3
  13.6 0.8 pair.1
  14.3 9.0 %all-to-all-start = ((bf16[16,16,512]{2,1,0:T(8,128)(2,1)}), bf16[16,16,512]{2,1,0:T(8,128)(2,1)S(1)}, u32[]{:S(2)}, u32[]{:S(2)}) async-start(bf16[16,16,512]{2,1,0:T(8,128)(2,1)} %bitcast.2), calls=%async_computation | async-start | bytes 524288 | tf_op jit(solution)/shard_map/all_to_all | solution.py:410
  23.3 0.0 copy-done.5
  23.4 0.0 copy-done.6
  23.4 0.5 prepare.1
  23.9 0.0 copy-start.7
  23.9 0.6 copy-done.7
  24.5 0.7 constant_dynamic-slice_fusion.1.frac
  25.2 0.9 constant_dynamic-slice_fusion.feats
  26.1 7.6 %all-to-all-done.spread = bf16[16,16,512]{2,1,0:T(8,128)(2,1)S(1)} async-done(((bf16[16,16,512]{2,1,0:T(8,128)(2,1)}), bf16[16,16,512]{2,1,0:T(8,128)(2,1)S(1)}, u32[]{:S(2)}, u32[]{:S(2)}) %all-to-all-start) | async-done | bytes 262176 | tf_op jit(solution)/shard_map/all_to_all | solution.py:410
  33.8 14.6 %all_to_all.20 = bf16[16,16,512]{2,1,0:T(8,128)(2,1)S(1)} all-to-all(bf16[16,16,512]{2,1,0:T(8,128)(2,1)S(1)} %panel.1), channel_id=1, replica_groups=mesh['xh'=2,'z'=8,'core'=2,'xl'=2,'y'=4] {'xh','z'}, dimensions={0} | all-to-all | bytes 524288 | tf_op jit(solution)/shard_map/all_to_all | solution.py:410
  48.4 0.0 copy-start.2
  48.4 1.1 %copies.1 = bf16[8,272,256]{2,1,0:T(8,128)(2,1)} custom-call(f32[1]{0:T(128)} %bitcast.core, bf16[256,512]{1,0:T(8,128)(2,1)S(1)} %bitcast.5, s32[3,256]{1,0:T(4,128)S(1)} %copy-done.5), custom_call_target="tpu_custom_call" | custom-call | flops 1000000 | bytes 1000000 | tf_op jit(solution)/shard_map/copies/pallas_call | solution.py:210
  49.5 4.2 %all-to-all-start.2 = ((bf16[8,272,256]{2,1,0:T(8,128)(2,1)}), bf16[8,272,256]{2,1,0:T(8,128)(2,1)S(1)}, u32[]{:S(2)}, u32[]{:S(2)}) async-start(bf16[8,272,256]{2,1,0:T(8,128)(2,1)} %copies.1), calls=%async_computation.2 | async-start | bytes 2228224 | tf_op jit(solution)/shard_map/all_to_all | solution.py:410
  53.7 3.4 %collective-permute-start.1 = (bf16[256,512]{1,0:T(8,128)(2,1)S(1)}, bf16[256,512]{1,0:T(8,128)(2,1)S(1)}, u32[]{:S(2)}, u32[]{:S(2)}) collective-permute-start(bf16[256,512]{1,0:T(8,128)(2,1)S(1)} %bitcast.6), channel_id=1, source_target_pairs={{0,8},{8,0},{1,9},{9,1},{2,10},{10,2},{3,11},{11,3},{4,12},{12,4},... | collective-permute-start | bytes 786440 | tf_op jit(solution)/shard_map/ppermute | solution.py:438
  57.1 1.2 %collective-permute-done.1.other = bf16[256,512]{1,0:T(8,128)(2,1)S(1)} collective-permute-done((bf16[256,512]{1,0:T(8,128)(2,1)S(1)}, bf16[256,512]{1,0:T(8,128)(2,1)S(1)}, u32[]{:S(2)}, u32[]{:S(2)}) %collective-permute-start.1) | collective-permute-done | bytes 262176 | tf_op jit(solution)/shard_map/ppermute | solution.py:438
  58.3 0.0 copy-start.8
  58.3 0.0 copy-done.2
  58.3 0.7 copy-done.8
  59.0 9.0 %forces.1.force = bf16[48,256]{1,0:T(8,128)(2,1)} custom-call(f32[1]{0:T(128)} %bitcast.core, f32[3,4096]{1,0:T(4,128)} %frac.4, s32[1,4096]{1,0:T(1,128)} %bitcast.9, bf16[4096,256]{1,0:T(8,128)(2,1)} %feats.5, bf16[4096,256]{1,0:T(8,128)(2,1)} %cot.3, s32[3,256]{1,0:T(4,128)} %miller.4, f32[8,256]{1,0:T(8,128)} %gain.3, bf16[256,512]{1,0:T(8,128)(2,1)} %bitcast.7, ...), custom_call_target="tpu_custom_call" | custom-call | flops 2097152000 | bytes 8388608 | tf_op jit(solution)/shard_map/forces/pallas_call | solution.py:259
  68.0 0.0 copy-start.4
  68.0 0.0 all-to-all-done.2.mine
  68.0 0.0 copy-start
  68.0 2.1 %collective-permute-start.2 = (bf16[8,272,256]{2,1,0:T(8,128)(2,1)S(1)}, bf16[8,272,256]{2,1,0:T(8,128)(2,1)S(1)}, u32[]{:S(2)}, u32[]{:S(2)}) collective-permute-start(bf16[8,272,256]{2,1,0:T(8,128)(2,1)S(1)} %all-to-all-done.2.mine), channel_id=1, source_target_pairs={{0,8},{8,0},{1,9},{9,1},{2,10},{10,2},{3,11},{11,3},{4,12},{12,4},... | collective-permute-start | bytes 3342344 | tf_op jit(solution)/shard_map/ppermute | solution.py:442
  70.2 1.6 %half.1 = (f32[256,256]{1,0:T(8,128)S(1)}, bf16[256,2048]{1,0:T(8,128)(2,1)S(1)}) custom-call(f32[3,256]{1,0:T(4,128)S(1)} %constant_dynamic-slice_fusion.1.frac, bf16[8,272,256]{2,1,0:T(8,128)(2,1)S(1)} %all-to-all-done.2.mine), custom_call_target="tpu_custom_call" | custom-call | flops 2000000000 | bytes 1000000 | tf_op jit(solution)/shard_map/half/pallas_call | solution.py:336
  71.8 0.0 copy-done
  71.8 0.8 collective-permute-done.2.other
  72.6 0.0 copy-start.1
  72.6 0.0 copy-done.4
  72.6 1.5 %share.1 = bf16[8,304,256]{2,1,0:T(8,128)(2,1)} custom-call(f32[256,256]{1,0:T(8,128)S(1)} %get-tuple-element.34.total, bf16[256,2048]{1,0:T(8,128)(2,1)S(1)} %get-tuple-element.35.table, bf16[8,272,256]{2,1,0:T(8,128)(2,1)S(1)} %collective-permute-done.2.other, bf16[256,256]{1,0:T(8,128)(2,1)S(1)} %constant_dynamic-slice_fusion.feats, ...), custom_call_target="tpu_custom_call" | custom-call | flops 1000000000 | bytes 1000000 | tf_op jit(solution)/shard_map/share/pallas_call | solution.py:364
  74.1 0.0 copy-done.1
  74.1 3.7 %all-to-all-start.3 = ((bf16[8,304,256]{2,1,0:T(8,128)(2,1)}), bf16[8,304,256]{2,1,0:T(8,128)(2,1)S(1)}, u32[]{:S(2)}, u32[]{:S(2)}) async-start(bf16[8,304,256]{2,1,0:T(8,128)(2,1)} %share.1), calls=%async_computation.3 | async-start | bytes 2490368 | tf_op jit(solution)/shard_map/all_to_all | solution.py:410
  77.8 15.8 %rest.1 = bf16[4096,256]{1,0:T(8,128)(2,1)} custom-call(f32[3,4096]{1,0:T(4,128)} %frac.4, bf16[4096,256]{1,0:T(8,128)(2,1)} %feats.5, bf16[8,272,256]{2,1,0:T(8,128)(2,1)} %copy-done, bf16[8,272,256]{2,1,0:T(8,128)(2,1)} %copy-done.1), custom_call_target="tpu_custom_call" | custom-call | flops 10000000000 | bytes 1000000 | tf_op jit(solution)/shard_map/rest/pallas_call | solution.py:392
  93.6 1.2 %all-to-all-done.3.parts = bf16[8,304,256]{2,1,0:T(8,128)(2,1)S(1)} async-done(((bf16[8,304,256]{2,1,0:T(8,128)(2,1)}), bf16[8,304,256]{2,1,0:T(8,128)(2,1)S(1)}, u32[]{:S(2)}, u32[]{:S(2)}) %all-to-all-start.3) | async-done | bytes 1245216 | tf_op jit(solution)/shard_map/all_to_all | solution.py:410
  94.9 1.7 %finish.1 = (bf16[4096,256]{1,0:T(8,128)(2,1)}, f32[3,4096]{1,0:T(4,128)}) custom-call(bf16[8,304,256]{2,1,0:T(8,128)(2,1)S(1)} %all-to-all-done.3.parts, bf16[4096,256]{1,0:T(8,128)(2,1)} %rest.1), custom_call_target="tpu_custom_call", output_to_operand_aliasing={{0}: (1, {})} | custom-call | flops 1000000 | bytes 1000000 | tf_op jit(solution)/shard_map/finish/pallas_call | solution.py:309
  (1 shorter events, 0.0 us)
Async XLA Ops:
  0.6 22.7 %copy-start.5 = (s32[3,256]{1,0:T(4,128)S(1)}, s32[3,256]{1,0:T(4,128)}, u32[]{:S(2)}) copy-start(s32[3,256]{1,0:T(4,128)} %miller.4) | copy-start | bytes 9220
  0.6 22.7 %copy-start.6 = (f32[16,256]{1,0:T(8,128)S(1)}, f32[16,256]{1,0:T(8,128)}, u32[]{:S(2)}) copy-start(f32[16,256]{1,0:T(8,128)} %filter_weight.1) | copy-start | bytes 49156
  8.0 4.6 %collective-permute-start = (bf16[256,512]{1,0:T(8,128)(2,1)}, bf16[256,512]{1,0:T(8,128)(2,1)S(1)}, u32[]{:S(2)}, u32[]{:S(2)}) collective-permute-start(bf16[256,512]{1,0:T(8,128)(2,1)} %get-tuple-element.23), channel_id=1, source_target_pairs={{0,8},{8,0},{1,9},{9,1},{2,10},{10,2},{3,11},{11,3},{4,12},{12,4},... | collective-permute-start | bytes 786440 | tf_op jit(solution)/shard_map/ppermute | solution.py:427
  12.6 0.9 copy-start.3
  14.3 19.5 %all-to-all-start = ((bf16[16,16,512]{2,1,0:T(8,128)(2,1)}), bf16[16,16,512]{2,1,0:T(8,128)(2,1)S(1)}, u32[]{:S(2)}, u32[]{:S(2)}) async-start(bf16[16,16,512]{2,1,0:T(8,128)(2,1)} %bitcast.2), calls=%async_computation | async-start | bytes 524288 | tf_op jit(solution)/shard_map/all_to_all | solution.py:410
  23.9 0.7 copy-start.7
  48.4 9.9 %copy-start.2 = (bf16[16,16,512]{2,1,0:T(8,128)(2,1)}, bf16[16,16,512]{2,1,0:T(8,128)(2,1)S(1)}, u32[]{:S(2)}) copy-start(bf16[16,16,512]{2,1,0:T(8,128)(2,1)S(1)} %all_to_all.20) | copy-start | bytes 786436
  49.5 18.5 %all-to-all-start.2 = ((bf16[8,272,256]{2,1,0:T(8,128)(2,1)}), bf16[8,272,256]{2,1,0:T(8,128)(2,1)S(1)}, u32[]{:S(2)}, u32[]{:S(2)}) async-start(bf16[8,272,256]{2,1,0:T(8,128)(2,1)} %copies.1), calls=%async_computation.2 | async-start | bytes 2228224 | tf_op jit(solution)/shard_map/all_to_all | solution.py:410
  53.7 4.6 %collective-permute-start.1 = (bf16[256,512]{1,0:T(8,128)(2,1)S(1)}, bf16[256,512]{1,0:T(8,128)(2,1)S(1)}, u32[]{:S(2)}, u32[]{:S(2)}) collective-permute-start(bf16[256,512]{1,0:T(8,128)(2,1)S(1)} %bitcast.6), channel_id=1, source_target_pairs={{0,8},{8,0},{1,9},{9,1},{2,10},{10,2},{3,11},{11,3},{4,12},{12,4},... | collective-permute-start | bytes 786440 | tf_op jit(solution)/shard_map/ppermute | solution.py:438
  58.3 0.7 copy-start.8
  68.0 4.6 %copy-start.4 = (bf16[48,256]{1,0:T(8,128)(2,1)S(1)}, bf16[48,256]{1,0:T(8,128)(2,1)}, u32[]{:S(2)}) copy-start(bf16[48,256]{1,0:T(8,128)(2,1)} %forces.1.force) | copy-start | bytes 73732
  68.0 3.8 %copy-start = (bf16[8,272,256]{2,1,0:T(8,128)(2,1)}, bf16[8,272,256]{2,1,0:T(8,128)(2,1)S(1)}, u32[]{:S(2)}) copy-start(bf16[8,272,256]{2,1,0:T(8,128)(2,1)S(1)} %all-to-all-done.2.mine) | copy-start | bytes 3342340
  68.0 4.5 %collective-permute-start.2 = (bf16[8,272,256]{2,1,0:T(8,128)(2,1)S(1)}, bf16[8,272,256]{2,1,0:T(8,128)(2,1)S(1)}, u32[]{:S(2)}, u32[]{:S(2)}) collective-permute-start(bf16[8,272,256]{2,1,0:T(8,128)(2,1)S(1)} %all-to-all-done.2.mine), channel_id=1, source_target_pairs={{0,8},{8,0},{1,9},{9,1},{2,10},{10,2},{3,11},{11,3},{4,12},{12,4},... | collective-permute-start | bytes 3342344 | tf_op jit(solution)/shard_map/ppermute | solution.py:442
  72.6 1.5 %copy-start.1 = (bf16[8,272,256]{2,1,0:T(8,128)(2,1)}, bf16[8,272,256]{2,1,0:T(8,128)(2,1)S(1)}, u32[]{:S(2)}) copy-start(bf16[8,272,256]{2,1,0:T(8,128)(2,1)S(1)} %collective-permute-done.2.other) | copy-start | bytes 3342340
  74.1 20.8 %all-to-all-start.3 = ((bf16[8,304,256]{2,1,0:T(8,128)(2,1)}), bf16[8,304,256]{2,1,0:T(8,128)(2,1)S(1)}, u32[]{:S(2)}, u32[]{:S(2)}) async-start(bf16[8,304,256]{2,1,0:T(8,128)(2,1)} %share.1), calls=%async_computation.3 | async-start | bytes 2490368 | tf_op jit(solution)/shard_map/all_to_all | solution.py:410

commit v4 on v3

--- a/solution.py
+++ b/solution.py
@@ -129,7 +129,7 @@
         give[...] = acc[kn:2 * kn, :].astype(jnp.bfloat16)
 
 
-def factors(core, frac, species, feats, cot, miller, gain, tile=1024):
+def factors(core, frac, species, feats, cot, miller, gain, tile=2048):
     n, ch = feats.shape
     kn = miller.shape[1]
     return pl.pallas_call(
@@ -375,14 +375,23 @@
 def rest_kernel(scale, frac, feats, mine, other, out):
     blocks = mine.shape[0]
     kn = mine.shape[1] - DEPTH
+    rows = 256
     place = places(frac[...]).T
-    for at in range(0, feats.shape[0], 256):
-        here = slice(at, at + 256)
-        total = jnp.zeros((256, feats.shape[1]), jnp.float32)
-        for b in range(blocks):
-            c, s = cos_sin(contract(place[here], mine[b, kn:kn + DEPTH, :], ((1,), (0,))))
-            total += contract(c, mine[b, 0:kn, :], ((1,), (0,)))
-            total += contract(s, other[b, 0:kn, :], ((1,), (0,)))
+    panels = [jnp.concatenate([p[b, 0:kn, :] for b in range(blocks)], axis=0) for p in (mine, other)]
+
+    def tables_at(at):
+        pairs = [
+            cos_sin(contract(place[at:at + rows], mine[b, kn:kn + DEPTH, :], ((1,), (0,)))) for b in range(blocks)
+        ]
+        return [jnp.concatenate(table, axis=1) for table in zip(*pairs)]
+
+    after = tables_at(0)
+    for at in range(0, feats.shape[0], rows):
+        here = slice(at, at + rows)
+        first, second = after
+        if at + rows < feats.shape[0]:
+            after = tables_at(at + rows)
+        total = contract(first, panels[0], ((1,), (0,))) + contract(second, panels[1], ((1,), (0,)))
         out[here, :] = (feats[here, :].astype(jnp.float32) + total * scale).astype(jnp.bfloat16)
 
 
@@ -453,7 +462,7 @@
     sizes = dict(mesh.shape)
     fine = Mesh(mesh.devices.reshape(2, sizes["dom"] // 4, 2, 2, sizes["ka"] // 2), ("xh", "z", "core", "xl", "y"))
     dom = ("xh", "z", "core")
-    placed = (P(None, dom), P(dom), P(dom, None), P(dom, None), P(None, ACROSS), P(), P())
+    placed = (P(None, dom), P(dom), P(dom, None), P(dom, None), P(None, ("xl", "y")), P(), P())
     return jax.shard_map(
         body,
         mesh=fine,

time: 97.2 us -> 97.2 us (level)
  Pallas kernels: 39.3 us -> 38.2 us
  waiting for transfers between devices: 12.2 us -> 13.2 us
    pallas_call x1, Pallas kernels: 15.8 us -> 14.7 us  [rest_of(): pl.pallas_call(functools.partial(rest_kernel, scale), grid=((n - start) /...]
    all_to_all x3, waiting for transfers between devices: 8.9 us -> 9.96 us  [across(): return lax.all_to_all(x, axes, 0, 0)]
  transfers between devices with their start and end apart: 6 -> 6, of which waited for: 5 -> 5; matrix products, arithmetic and copies ran while one was open for 2% -> 2% of each run, Pallas kernels for 28% -> 27%
where the time goes in v4:
time: 97.2 us; the launch traced here: 96.7 us
  Pallas kernels  38.2 us (39%)
  starting transfers between devices  25.8 us (27%)
  blocking collectives  14.6 us (15%)
  waiting for transfers between devices  13.2 us (14%)
  local copies, waits for them, and re-layouts  3.91 us (4%)
    all_to_all x3, starting transfers between devices, across(): return lax.all_to_all(x, axes, 0, 0)  17 us
    pallas_call x1, Pallas kernels, rest_of(): pl.pallas_call(functools.partial(rest_kernel, scale), grid=((n - start) /...  14.7 us
    all_to_all x1, blocking collectives, across(): return lax.all_to_all(x, axes, 0, 0)  14.6 us
    all_to_all x3, waiting for transfers between devices, across(): return lax.all_to_all(x, axes, 0, 0)  9.96 us
    pallas_call x1, Pallas kernels, forces_of(): pl.pallas_call(functools.partial(forces_kernel, scale), grid=(n // tile,)...  9.04 us
    pallas_call x1, Pallas kernels, factors(): pl.pallas_call(factors_kernel, grid=(n // tile,), in_specs=[SCALAR, pl.Bl...  7.32 us
    ppermute x1, starting transfers between devices, body(): other = lax.ppermute(mine, 'core', SWAP)  3.4 us
    ppermute x1, starting transfers between devices, body(): pair = pair_of(keep, lax.ppermute(give, 'core', SWAP))  3.24 us
  transfers between devices with their start and end apart: 6, of which 5 were waited for; matrix products, arithmetic and copies ran while one was open for 2% of the time, Pallas kernels for 27%

profile of v4, /device:TPU:1, one launch (start us, length us, event | category | flops | bytes accessed | tf_op | source)
XLA Modules:
  0.0 96.7 jit_solution(9623464411262952604)
XLA Ops:
  0.6 0.0 copy-start.5
  0.6 0.0 copy-start.6
  0.7 7.3 %factors.1 = (bf16[256,512]{1,0:T(8,128)(2,1)}, bf16[256,512]{1,0:T(8,128)(2,1)}) custom-call(f32[1]{0:T(128)} %bitcast.core, f32[3,4096]{1,0:T(4,128)} %frac.4, s32[1,4096]{1,0:T(1,128)} %bitcast.8, bf16[4096,256]{1,0:T(8,128)(2,1)} %feats.5, bf16[4096,256]{1,0:T(8,128)(2,1)} %cot.3, s32[3,256]{1,0:T(4,128)} %miller.4, f32[8,256]{1,0:T(8,128)} %gain.3), custom_call_target="tpu_custom_call" | custom-call | flops 2147483648 | bytes 12582912 | tf_op jit(solution)/shard_map/factors/pallas_call | solution.py:135
  8.0 3.2 %collective-permute-start = (bf16[256,512]{1,0:T(8,128)(2,1)}, bf16[256,512]{1,0:T(8,128)(2,1)S(1)}, u32[]{:S(2)}, u32[]{:S(2)}) collective-permute-start(bf16[256,512]{1,0:T(8,128)(2,1)} %get-tuple-element.23), channel_id=1, source_target_pairs={{0,8},{8,0},{1,9},{9,1},{2,10},{10,2},{3,11},{11,3},{4,12},{12,4},... | collective-permute-start | bytes 786440 | tf_op jit(solution)/shard_map/ppermute | solution.py:436
  11.2 1.4 %collective-permute-done.got = bf16[256,512]{1,0:T(8,128)(2,1)S(1)} collective-permute-done((bf16[256,512]{1,0:T(8,128)(2,1)}, bf16[256,512]{1,0:T(8,128)(2,1)S(1)}, u32[]{:S(2)}, u32[]{:S(2)}) %collective-permute-start) | collective-permute-done | bytes 262176 | tf_op jit(solution)/shard_map/ppermute | solution.py:436
  12.6 0.0 copy-start.3
  12.6 0.9 copy-done.3
  13.5 0.8 pair.1
  14.3 9.0 %all-to-all-start = ((bf16[16,16,512]{2,1,0:T(8,128)(2,1)}), bf16[16,16,512]{2,1,0:T(8,128)(2,1)S(1)}, u32[]{:S(2)}, u32[]{:S(2)}) async-start(bf16[16,16,512]{2,1,0:T(8,128)(2,1)} %bitcast.2), calls=%async_computation | async-start | bytes 524288 | tf_op jit(solution)/shard_map/all_to_all | solution.py:419
  23.3 0.0 copy-done.5
  23.3 0.0 copy-done.6
  23.4 0.5 prepare.1
  23.9 0.0 copy-start.7
  23.9 0.6 copy-done.7
  24.5 0.7 constant_dynamic-slice_fusion.1.frac
  25.2 0.9 constant_dynamic-slice_fusion.feats
  26.1 7.6 %all-to-all-done.spread = bf16[16,16,512]{2,1,0:T(8,128)(2,1)S(1)} async-done(((bf16[16,16,512]{2,1,0:T(8,128)(2,1)}), bf16[16,16,512]{2,1,0:T(8,128)(2,1)S(1)}, u32[]{:S(2)}, u32[]{:S(2)}) %all-to-all-start) | async-done | bytes 262176 | tf_op jit(solution)/shard_map/all_to_all | solution.py:419
  33.8 14.6 %all_to_all.20 = bf16[16,16,512]{2,1,0:T(8,128)(2,1)S(1)} all-to-all(bf16[16,16,512]{2,1,0:T(8,128)(2,1)S(1)} %panel.1), channel_id=1, replica_groups=mesh['xh'=2,'z'=8,'core'=2,'xl'=2,'y'=4] {'xh','z'}, dimensions={0} | all-to-all | bytes 524288 | tf_op jit(solution)/shard_map/all_to_all | solution.py:419
  48.4 0.0 copy-start.2
  48.4 1.1 %copies.1 = bf16[8,272,256]{2,1,0:T(8,128)(2,1)} custom-call(f32[1]{0:T(128)} %bitcast.core, bf16[256,512]{1,0:T(8,128)(2,1)S(1)} %bitcast.5, s32[3,256]{1,0:T(4,128)S(1)} %copy-done.5), custom_call_target="tpu_custom_call" | custom-call | flops 1000000 | bytes 1000000 | tf_op jit(solution)/shard_map/copies/pallas_call | solution.py:210
  49.5 4.2 %all-to-all-start.2 = ((bf16[8,272,256]{2,1,0:T(8,128)(2,1)}), bf16[8,272,256]{2,1,0:T(8,128)(2,1)S(1)}, u32[]{:S(2)}, u32[]{:S(2)}) async-start(bf16[8,272,256]{2,1,0:T(8,128)(2,1)} %copies.1), calls=%async_computation.2 | async-start | bytes 2228224 | tf_op jit(solution)/shard_map/all_to_all | solution.py:419
  53.7 3.4 %collective-permute-start.1 = (bf16[256,512]{1,0:T(8,128)(2,1)S(1)}, bf16[256,512]{1,0:T(8,128)(2,1)S(1)}, u32[]{:S(2)}, u32[]{:S(2)}) collective-permute-start(bf16[256,512]{1,0:T(8,128)(2,1)S(1)} %bitcast.6), channel_id=1, source_target_pairs={{0,8},{8,0},{1,9},{9,1},{2,10},{10,2},{3,11},{11,3},{4,12},{12,4},... | collective-permute-start | bytes 786440 | tf_op jit(solution)/shard_map/ppermute | solution.py:447
  57.1 1.2 %collective-permute-done.1.other = bf16[256,512]{1,0:T(8,128)(2,1)S(1)} collective-permute-done((bf16[256,512]{1,0:T(8,128)(2,1)S(1)}, bf16[256,512]{1,0:T(8,128)(2,1)S(1)}, u32[]{:S(2)}, u32[]{:S(2)}) %collective-permute-start.1) | collective-permute-done | bytes 262176 | tf_op jit(solution)/shard_map/ppermute | solution.py:447
  58.3 0.0 copy-start.8
  58.3 0.0 copy-done.2
  58.3 0.7 copy-done.8
  59.0 9.0 %forces.1.force = bf16[48,256]{1,0:T(8,128)(2,1)} custom-call(f32[1]{0:T(128)} %bitcast.core, f32[3,4096]{1,0:T(4,128)} %frac.4, s32[1,4096]{1,0:T(1,128)} %bitcast.9, bf16[4096,256]{1,0:T(8,128)(2,1)} %feats.5, bf16[4096,256]{1,0:T(8,128)(2,1)} %cot.3, s32[3,256]{1,0:T(4,128)} %miller.4, f32[8,256]{1,0:T(8,128)} %gain.3, bf16[256,512]{1,0:T(8,128)(2,1)} %bitcast.7, ...), custom_call_target="tpu_custom_call" | custom-call | flops 2097152000 | bytes 8388608 | tf_op jit(solution)/shard_map/forces/pallas_call | solution.py:259
  68.0 0.0 copy-start.4
  68.0 0.0 all-to-all-done.2.mine
  68.0 0.0 copy-start
  68.0 2.1 %collective-permute-start.2 = (bf16[8,272,256]{2,1,0:T(8,128)(2,1)S(1)}, bf16[8,272,256]{2,1,0:T(8,128)(2,1)S(1)}, u32[]{:S(2)}, u32[]{:S(2)}) collective-permute-start(bf16[8,272,256]{2,1,0:T(8,128)(2,1)S(1)} %all-to-all-done.2.mine), channel_id=1, source_target_pairs={{0,8},{8,0},{1,9},{9,1},{2,10},{10,2},{3,11},{11,3},{4,12},{12,4},... | collective-permute-start | bytes 3342344 | tf_op jit(solution)/shard_map/ppermute | solution.py:451
  70.2 1.6 %half.1 = (f32[256,256]{1,0:T(8,128)S(1)}, bf16[256,2048]{1,0:T(8,128)(2,1)S(1)}) custom-call(f32[3,256]{1,0:T(4,128)S(1)} %constant_dynamic-slice_fusion.1.frac, bf16[8,272,256]{2,1,0:T(8,128)(2,1)S(1)} %all-to-all-done.2.mine), custom_call_target="tpu_custom_call" | custom-call | flops 2000000000 | bytes 1000000 | tf_op jit(solution)/shard_map/half/pallas_call | solution.py:336
  71.8 0.0 copy-done
  71.8 0.8 collective-permute-done.2.other
  72.6 0.0 copy-start.1
  72.6 0.0 copy-done.4
  72.6 1.5 %share.1 = bf16[8,304,256]{2,1,0:T(8,128)(2,1)} custom-call(f32[256,256]{1,0:T(8,128)S(1)} %get-tuple-element.34.total, bf16[256,2048]{1,0:T(8,128)(2,1)S(1)} %get-tuple-element.35.table, bf16[8,272,256]{2,1,0:T(8,128)(2,1)S(1)} %collective-permute-done.2.other, bf16[256,256]{1,0:T(8,128)(2,1)S(1)} %constant_dynamic-slice_fusion.feats, ...), custom_call_target="tpu_custom_call" | custom-call | flops 1000000000 | bytes 1000000 | tf_op jit(solution)/shard_map/share/pallas_call | solution.py:364
  74.1 0.0 copy-done.1
  74.1 3.7 %all-to-all-start.3 = ((bf16[8,304,256]{2,1,0:T(8,128)(2,1)}), bf16[8,304,256]{2,1,0:T(8,128)(2,1)S(1)}, u32[]{:S(2)}, u32[]{:S(2)}) async-start(bf16[8,304,256]{2,1,0:T(8,128)(2,1)} %share.1), calls=%async_computation.3 | async-start | bytes 2490368 | tf_op jit(solution)/shard_map/all_to_all | solution.py:419
  77.8 14.7 %rest.1 = bf16[4096,256]{1,0:T(8,128)(2,1)} custom-call(f32[3,4096]{1,0:T(4,128)} %frac.4, bf16[4096,256]{1,0:T(8,128)(2,1)} %feats.5, bf16[8,272,256]{2,1,0:T(8,128)(2,1)} %copy-done, bf16[8,272,256]{2,1,0:T(8,128)(2,1)} %copy-done.1), custom_call_target="tpu_custom_call" | custom-call | flops 10000000000 | bytes 1000000 | tf_op jit(solution)/shard_map/rest/pallas_call | solution.py:401
  92.6 2.3 %all-to-all-done.3.parts = bf16[8,304,256]{2,1,0:T(8,128)(2,1)S(1)} async-done(((bf16[8,304,256]{2,1,0:T(8,128)(2,1)}), bf16[8,304,256]{2,1,0:T(8,128)(2,1)S(1)}, u32[]{:S(2)}, u32[]{:S(2)}) %all-to-all-start.3) | async-done | bytes 1245216 | tf_op jit(solution)/shard_map/all_to_all | solution.py:419
  94.9 1.7 %finish.1 = (bf16[4096,256]{1,0:T(8,128)(2,1)}, f32[3,4096]{1,0:T(4,128)}) custom-call(bf16[8,304,256]{2,1,0:T(8,128)(2,1)S(1)} %all-to-all-done.3.parts, bf16[4096,256]{1,0:T(8,128)(2,1)} %rest.1), custom_call_target="tpu_custom_call", output_to_operand_aliasing={{0}: (1, {})} | custom-call | flops 1000000 | bytes 1000000 | tf_op jit(solution)/shard_map/finish/pallas_call | solution.py:309
  (1 shorter events, 0.0 us)
Async XLA Ops:
  0.6 22.7 %copy-start.5 = (s32[3,256]{1,0:T(4,128)S(1)}, s32[3,256]{1,0:T(4,128)}, u32[]{:S(2)}) copy-start(s32[3,256]{1,0:T(4,128)} %miller.4) | copy-start | bytes 9220
  0.6 22.7 %copy-start.6 = (f32[16,256]{1,0:T(8,128)S(1)}, f32[16,256]{1,0:T(8,128)}, u32[]{:S(2)}) copy-start(f32[16,256]{1,0:T(8,128)} %filter_weight.1) | copy-start | bytes 49156
  8.0 4.6 %collective-permute-start = (bf16[256,512]{1,0:T(8,128)(2,1)}, bf16[256,512]{1,0:T(8,128)(2,1)S(1)}, u32[]{:S(2)}, u32[]{:S(2)}) collective-permute-start(bf16[256,512]{1,0:T(8,128)(2,1)} %get-tuple-element.23), channel_id=1, source_target_pairs={{0,8},{8,0},{1,9},{9,1},{2,10},{10,2},{3,11},{11,3},{4,12},{12,4},... | collective-permute-start | bytes 786440 | tf_op jit(solution)/shard_map/ppermute | solution.py:436
  12.6 0.9 copy-start.3
  14.3 19.5 %all-to-all-start = ((bf16[16,16,512]{2,1,0:T(8,128)(2,1)}), bf16[16,16,512]{2,1,0:T(8,128)(2,1)S(1)}, u32[]{:S(2)}, u32[]{:S(2)}) async-start(bf16[16,16,512]{2,1,0:T(8,128)(2,1)} %bitcast.2), calls=%async_computation | async-start | bytes 524288 | tf_op jit(solution)/shard_map/all_to_all | solution.py:419
  23.9 0.7 copy-start.7
  48.4 9.9 %copy-start.2 = (bf16[16,16,512]{2,1,0:T(8,128)(2,1)}, bf16[16,16,512]{2,1,0:T(8,128)(2,1)S(1)}, u32[]{:S(2)}) copy-start(bf16[16,16,512]{2,1,0:T(8,128)(2,1)S(1)} %all_to_all.20) | copy-start | bytes 786436
  49.5 18.5 %all-to-all-start.2 = ((bf16[8,272,256]{2,1,0:T(8,128)(2,1)}), bf16[8,272,256]{2,1,0:T(8,128)(2,1)S(1)}, u32[]{:S(2)}, u32[]{:S(2)}) async-start(bf16[8,272,256]{2,1,0:T(8,128)(2,1)} %copies.1), calls=%async_computation.2 | async-start | bytes 2228224 | tf_op jit(solution)/shard_map/all_to_all | solution.py:419
  53.7 4.6 %collective-permute-start.1 = (bf16[256,512]{1,0:T(8,128)(2,1)S(1)}, bf16[256,512]{1,0:T(8,128)(2,1)S(1)}, u32[]{:S(2)}, u32[]{:S(2)}) collective-permute-start(bf16[256,512]{1,0:T(8,128)(2,1)S(1)} %bitcast.6), channel_id=1, source_target_pairs={{0,8},{8,0},{1,9},{9,1},{2,10},{10,2},{3,11},{11,3},{4,12},{12,4},... | collective-permute-start | bytes 786440 | tf_op jit(solution)/shard_map/ppermute | solution.py:447
  58.3 0.7 copy-start.8
  68.0 4.6 %copy-start.4 = (bf16[48,256]{1,0:T(8,128)(2,1)S(1)}, bf16[48,256]{1,0:T(8,128)(2,1)}, u32[]{:S(2)}) copy-start(bf16[48,256]{1,0:T(8,128)(2,1)} %forces.1.force) | copy-start | bytes 73732
  68.0 3.8 %copy-start = (bf16[8,272,256]{2,1,0:T(8,128)(2,1)}, bf16[8,272,256]{2,1,0:T(8,128)(2,1)S(1)}, u32[]{:S(2)}) copy-start(bf16[8,272,256]{2,1,0:T(8,128)(2,1)S(1)} %all-to-all-done.2.mine) | copy-start | bytes 3342340
  68.0 4.5 %collective-permute-start.2 = (bf16[8,272,256]{2,1,0:T(8,128)(2,1)S(1)}, bf16[8,272,256]{2,1,0:T(8,128)(2,1)S(1)}, u32[]{:S(2)}, u32[]{:S(2)}) collective-permute-start(bf16[8,272,256]{2,1,0:T(8,128)(2,1)S(1)} %all-to-all-done.2.mine), channel_id=1, source_target_pairs={{0,8},{8,0},{1,9},{9,1},{2,10},{10,2},{3,11},{11,3},{4,12},{12,4},... | collective-permute-start | bytes 3342344 | tf_op jit(solution)/shard_map/ppermute | solution.py:451
  72.6 1.5 %copy-start.1 = (bf16[8,272,256]{2,1,0:T(8,128)(2,1)}, bf16[8,272,256]{2,1,0:T(8,128)(2,1)S(1)}, u32[]{:S(2)}) copy-start(bf16[8,272,256]{2,1,0:T(8,128)(2,1)S(1)} %collective-permute-done.2.other) | copy-start | bytes 3342340
  74.1 20.8 %all-to-all-start.3 = ((bf16[8,304,256]{2,1,0:T(8,128)(2,1)}), bf16[8,304,256]{2,1,0:T(8,128)(2,1)S(1)}, u32[]{:S(2)}, u32[]{:S(2)}) async-start(bf16[8,304,256]{2,1,0:T(8,128)(2,1)} %share.1), calls=%async_computation.3 | async-start | bytes 2490368 | tf_op jit(solution)/shard_map/all_to_all | solution.py:419

commit v5 on v4

--- a/solution.py
+++ b/solution.py
@@ -196,13 +196,19 @@
     )(where, spread, weights)
 
 
-def copies_kernel(core, mine, miller, out):
-    blocks, _, ch = out.shape
-    kn = miller.shape[1]
-    steps = steps_of(miller[...], core[0])
-    for i in range(blocks):
-        out[i, 0:kn, :] = mine[:, :ch]
-        out[i, kn:kn + DEPTH, :] = steps
+def send_all(block, out, sems):
+    copies = [pltpu.make_async_copy(block, out.at[b], sems.at[b]) for b in range(out.shape[0])]
+    for copy in copies:
+        copy.start()
+    for copy in copies:
+        copy.wait()
+
+
+def copies_kernel(core, mine, miller, out, block, sems):
+    kn = miller.shape[1]
+    block[0:kn, :] = mine[:, :block.shape[1]]
+    block[kn:kn + DEPTH, :] = steps_of(miller[...], core[0])
+    send_all(block, out, sems)
 
 
 def copies_of(core, mine, miller, width, blocks):
@@ -210,8 +216,12 @@
     return pl.pallas_call(
         copies_kernel,
         in_specs=[SCALAR, WHOLE, WHOLE],
-        out_specs=WHOLE,
+        out_specs=FAR,
         out_shape=jax.ShapeDtypeStruct((blocks, kn + DEPTH, width), jnp.bfloat16),
+        scratch_shapes=[
+            pltpu.VMEM((kn + DEPTH, width), jnp.bfloat16),
+            pltpu.SemaphoreType.DMA((blocks,)),
+        ],
         compiler_params=params(6),
         cost_estimate=cost(10**6, 10**6),
         name="copies",
@@ -347,16 +357,16 @@
     )(frac, mine)
 
 
-def share_kernel(scale, total, table, other, feats, force, out):
+def share_kernel(scale, total, table, other, feats, force, out, block, sems):
     kn = other.shape[1] - DEPTH
     share = feats.shape[0]
     sums = total[...]
     for b in range(other.shape[0]):
         sums += contract(table[:, b * kn:(b + 1) * kn], other[b, 0:kn, :], ((1,), (0,)))
     rows = (feats[...].astype(jnp.float32) + sums * scale).astype(jnp.bfloat16)
-    for b in range(out.shape[0]):
-        out[b, 0:share, :] = rows
-        out[b, share:, :] = force[...]
+    block[0:share, :] = rows
+    block[share:, :] = force[...]
+    send_all(block, out, sems)
 
 
 def share_of(total, table, other, feats, force, scale):
@@ -364,8 +374,12 @@
     return pl.pallas_call(
         functools.partial(share_kernel, scale),
         in_specs=[WHOLE] * 5,
-        out_specs=WHOLE,
+        out_specs=FAR,
         out_shape=jax.ShapeDtypeStruct((other.shape[0], share + force.shape[0], ch), jnp.bfloat16),
+        scratch_shapes=[
+            pltpu.VMEM((share + force.shape[0], ch), jnp.bfloat16),
+            pltpu.SemaphoreType.DMA((other.shape[0],)),
+        ],
         compiler_params=params(8),
         cost_estimate=cost(10**9, 10**6),
         name="share",

time: 97.2 us -> 97.3 us (level)
  no operation moved by 1% of the time
where the time goes in v5:
time: 97.3 us; the launch traced here: 96.9 us
  Pallas kernels  38.4 us (39%)
  starting transfers between devices  25.8 us (27%)
  blocking collectives  14.6 us (15%)
  waiting for transfers between devices  13.2 us (14%)
  local copies, waits for them, and re-layouts  3.91 us (4%)
    all_to_all x3, starting transfers between devices, across(): return lax.all_to_all(x, axes, 0, 0)  17 us
    pallas_call x1, Pallas kernels, rest_of(): pl.pallas_call(functools.partial(rest_kernel, scale), grid=((n - start) /...  14.7 us
    all_to_all x1, blocking collectives, across(): return lax.all_to_all(x, axes, 0, 0)  14.6 us
    all_to_all x3, waiting for transfers between devices, across(): return lax.all_to_all(x, axes, 0, 0)  9.95 us
    pallas_call x1, Pallas kernels, forces_of(): pl.pallas_call(functools.partial(forces_kernel, scale), grid=(n // tile,)...  9.04 us
    pallas_call x1, Pallas kernels, factors(): pl.pallas_call(factors_kernel, grid=(n // tile,), in_specs=[SCALAR, pl.Bl...  7.32 us
    ppermute x1, starting transfers between devices, body(): other = lax.ppermute(mine, 'core', SWAP)  3.4 us
    ppermute x1, starting transfers between devices, body(): pair = pair_of(keep, lax.ppermute(give, 'core', SWAP))  3.24 us
  transfers between devices with their start and end apart: 6, of which 5 were waited for; matrix products, arithmetic and copies ran while one was open for 2% of the time, Pallas kernels for 27%

profile of v5, /device:TPU:1, one launch (start us, length us, event | category | flops | bytes accessed | tf_op | source)
XLA Modules:
  0.0 96.9 jit_solution(12234483172597773793)
XLA Ops:
  0.6 0.0 copy-start.5
  0.6 0.0 copy-start.6
  0.7 7.3 %factors.1 = (bf16[256,512]{1,0:T(8,128)(2,1)}, bf16[256,512]{1,0:T(8,128)(2,1)}) custom-call(f32[1]{0:T(128)} %bitcast.core, f32[3,4096]{1,0:T(4,128)} %frac.4, s32[1,4096]{1,0:T(1,128)} %bitcast.8, bf16[4096,256]{1,0:T(8,128)(2,1)} %feats.5, bf16[4096,256]{1,0:T(8,128)(2,1)} %cot.3, s32[3,256]{1,0:T(4,128)} %miller.4, f32[8,256]{1,0:T(8,128)} %gain.3), custom_call_target="tpu_custom_call" | custom-call | flops 2147483648 | bytes 12582912 | tf_op jit(solution)/shard_map/factors/pallas_call | solution.py:135
  8.0 3.2 %collective-permute-start = (bf16[256,512]{1,0:T(8,128)(2,1)}, bf16[256,512]{1,0:T(8,128)(2,1)S(1)}, u32[]{:S(2)}, u32[]{:S(2)}) collective-permute-start(bf16[256,512]{1,0:T(8,128)(2,1)} %get-tuple-element.23), channel_id=1, source_target_pairs={{0,8},{8,0},{1,9},{9,1},{2,10},{10,2},{3,11},{11,3},{4,12},{12,4},... | collective-permute-start | bytes 786440 | tf_op jit(solution)/shard_map/ppermute | solution.py:450
  11.2 1.4 %collective-permute-done.got = bf16[256,512]{1,0:T(8,128)(2,1)S(1)} collective-permute-done((bf16[256,512]{1,0:T(8,128)(2,1)}, bf16[256,512]{1,0:T(8,128)(2,1)S(1)}, u32[]{:S(2)}, u32[]{:S(2)}) %collective-permute-start) | collective-permute-done | bytes 262176 | tf_op jit(solution)/shard_map/ppermute | solution.py:450
  12.6 0.0 copy-start.3
  12.6 0.9 copy-done.3
  13.5 0.8 pair.1
  14.3 9.0 %all-to-all-start = ((bf16[16,16,512]{2,1,0:T(8,128)(2,1)}), bf16[16,16,512]{2,1,0:T(8,128)(2,1)S(1)}, u32[]{:S(2)}, u32[]{:S(2)}) async-start(bf16[16,16,512]{2,1,0:T(8,128)(2,1)} %bitcast.2), calls=%async_computation | async-start | bytes 524288 | tf_op jit(solution)/shard_map/all_to_all | solution.py:433
  23.3 0.0 copy-done.5
  23.3 0.0 copy-done.6
  23.4 0.5 prepare.1
  23.9 0.0 copy-start.7
  23.9 0.6 copy-done.7
  24.5 0.7 constant_dynamic-slice_fusion.1.frac
  25.2 0.9 constant_dynamic-slice_fusion.feats
  26.1 7.6 %all-to-all-done.spread = bf16[16,16,512]{2,1,0:T(8,128)(2,1)S(1)} async-done(((bf16[16,16,512]{2,1,0:T(8,128)(2,1)}), bf16[16,16,512]{2,1,0:T(8,128)(2,1)S(1)}, u32[]{:S(2)}, u32[]{:S(2)}) %all-to-all-start) | async-done | bytes 262176 | tf_op jit(solution)/shard_map/all_to_all | solution.py:433
  33.8 14.6 %all_to_all.20 = bf16[16,16,512]{2,1,0:T(8,128)(2,1)S(1)} all-to-all(bf16[16,16,512]{2,1,0:T(8,128)(2,1)S(1)} %panel.1), channel_id=1, replica_groups=mesh['xh'=2,'z'=8,'core'=2,'xl'=2,'y'=4] {'xh','z'}, dimensions={0} | all-to-all | bytes 524288 | tf_op jit(solution)/shard_map/all_to_all | solution.py:433
  48.4 0.0 copy-start.2
  48.4 1.1 %copies.1 = bf16[8,272,256]{2,1,0:T(8,128)(2,1)} custom-call(f32[1]{0:T(128)} %bitcast.core, bf16[256,512]{1,0:T(8,128)(2,1)S(1)} %bitcast.5, s32[3,256]{1,0:T(4,128)S(1)} %copy-done.5), custom_call_target="tpu_custom_call" | custom-call | flops 1000000 | bytes 1000000 | tf_op jit(solution)/shard_map/copies/pallas_call | solution.py:216
  49.6 4.2 %all-to-all-start.2 = ((bf16[8,272,256]{2,1,0:T(8,128)(2,1)}), bf16[8,272,256]{2,1,0:T(8,128)(2,1)S(1)}, u32[]{:S(2)}, u32[]{:S(2)}) async-start(bf16[8,272,256]{2,1,0:T(8,128)(2,1)} %copies.1), calls=%async_computation.2 | async-start | bytes 2228224 | tf_op jit(solution)/shard_map/all_to_all | solution.py:433
  53.8 3.4 %collective-permute-start.1 = (bf16[256,512]{1,0:T(8,128)(2,1)S(1)}, bf16[256,512]{1,0:T(8,128)(2,1)S(1)}, u32[]{:S(2)}, u32[]{:S(2)}) collective-permute-start(bf16[256,512]{1,0:T(8,128)(2,1)S(1)} %bitcast.6), channel_id=1, source_target_pairs={{0,8},{8,0},{1,9},{9,1},{2,10},{10,2},{3,11},{11,3},{4,12},{12,4},... | collective-permute-start | bytes 786440 | tf_op jit(solution)/shard_map/ppermute | solution.py:461
  57.2 1.2 %collective-permute-done.1.other = bf16[256,512]{1,0:T(8,128)(2,1)S(1)} collective-permute-done((bf16[256,512]{1,0:T(8,128)(2,1)S(1)}, bf16[256,512]{1,0:T(8,128)(2,1)S(1)}, u32[]{:S(2)}, u32[]{:S(2)}) %collective-permute-start.1) | collective-permute-done | bytes 262176 | tf_op jit(solution)/shard_map/ppermute | solution.py:461
  58.4 0.0 copy-start.8
  58.4 0.0 copy-done.2
  58.4 0.7 copy-done.8
  59.1 9.0 %forces.1.force = bf16[48,256]{1,0:T(8,128)(2,1)} custom-call(f32[1]{0:T(128)} %bitcast.core, f32[3,4096]{1,0:T(4,128)} %frac.4, s32[1,4096]{1,0:T(1,128)} %bitcast.9, bf16[4096,256]{1,0:T(8,128)(2,1)} %feats.5, bf16[4096,256]{1,0:T(8,128)(2,1)} %cot.3, s32[3,256]{1,0:T(4,128)} %miller.4, f32[8,256]{1,0:T(8,128)} %gain.3, bf16[256,512]{1,0:T(8,128)(2,1)} %bitcast.7, ...), custom_call_target="tpu_custom_call" | custom-call | flops 2097152000 | bytes 8388608 | tf_op jit(solution)/shard_map/forces/pallas_call | solution.py:269
  68.1 0.0 copy-start.4
  68.1 0.0 all-to-all-done.2.mine
  68.1 0.0 copy-start
  68.1 2.1 %collective-permute-start.2 = (bf16[8,272,256]{2,1,0:T(8,128)(2,1)S(1)}, bf16[8,272,256]{2,1,0:T(8,128)(2,1)S(1)}, u32[]{:S(2)}, u32[]{:S(2)}) collective-permute-start(bf16[8,272,256]{2,1,0:T(8,128)(2,1)S(1)} %all-to-all-done.2.mine), channel_id=1, source_target_pairs={{0,8},{8,0},{1,9},{9,1},{2,10},{10,2},{3,11},{11,3},{4,12},{12,4},... | collective-permute-start | bytes 3342344 | tf_op jit(solution)/shard_map/ppermute | solution.py:465
  70.3 1.6 %half.1 = (f32[256,256]{1,0:T(8,128)S(1)}, bf16[256,2048]{1,0:T(8,128)(2,1)S(1)}) custom-call(f32[3,256]{1,0:T(4,128)S(1)} %constant_dynamic-slice_fusion.1.frac, bf16[8,272,256]{2,1,0:T(8,128)(2,1)S(1)} %all-to-all-done.2.mine), custom_call_target="tpu_custom_call" | custom-call | flops 2000000000 | bytes 1000000 | tf_op jit(solution)/shard_map/half/pallas_call | solution.py:346
  71.9 0.0 copy-done
  71.9 0.8 collective-permute-done.2.other
  72.7 0.0 copy-start.1
  72.7 0.0 copy-done.4
  72.7 1.6 %share.1 = bf16[8,304,256]{2,1,0:T(8,128)(2,1)} custom-call(f32[256,256]{1,0:T(8,128)S(1)} %get-tuple-element.34.total, bf16[256,2048]{1,0:T(8,128)(2,1)S(1)} %get-tuple-element.35.table, bf16[8,272,256]{2,1,0:T(8,128)(2,1)S(1)} %collective-permute-done.2.other, bf16[256,256]{1,0:T(8,128)(2,1)S(1)} %constant_dynamic-slice_fusion.feats, ...), custom_call_target="tpu_custom_call" | custom-call | flops 1000000000 | bytes 1000000 | tf_op jit(solution)/shard_map/share/pallas_call | solution.py:374
  74.2 0.0 copy-done.1
  74.2 3.8 %all-to-all-start.3 = ((bf16[8,304,256]{2,1,0:T(8,128)(2,1)}), bf16[8,304,256]{2,1,0:T(8,128)(2,1)S(1)}, u32[]{:S(2)}, u32[]{:S(2)}) async-start(bf16[8,304,256]{2,1,0:T(8,128)(2,1)} %share.1), calls=%async_computation.3 | async-start | bytes 2490368 | tf_op jit(solution)/shard_map/all_to_all | solution.py:433
  78.0 14.7 %rest.1 = bf16[4096,256]{1,0:T(8,128)(2,1)} custom-call(f32[3,4096]{1,0:T(4,128)} %frac.4, bf16[4096,256]{1,0:T(8,128)(2,1)} %feats.5, bf16[8,272,256]{2,1,0:T(8,128)(2,1)} %copy-done, bf16[8,272,256]{2,1,0:T(8,128)(2,1)} %copy-done.1), custom_call_target="tpu_custom_call" | custom-call | flops 10000000000 | bytes 1000000 | tf_op jit(solution)/shard_map/rest/pallas_call | solution.py:415
  92.7 2.3 %all-to-all-done.3.parts = bf16[8,304,256]{2,1,0:T(8,128)(2,1)S(1)} async-done(((bf16[8,304,256]{2,1,0:T(8,128)(2,1)}), bf16[8,304,256]{2,1,0:T(8,128)(2,1)S(1)}, u32[]{:S(2)}, u32[]{:S(2)}) %all-to-all-start.3) | async-done | bytes 1245216 | tf_op jit(solution)/shard_map/all_to_all | solution.py:433
  95.0 1.7 %finish.1 = (bf16[4096,256]{1,0:T(8,128)(2,1)}, f32[3,4096]{1,0:T(4,128)}) custom-call(bf16[8,304,256]{2,1,0:T(8,128)(2,1)S(1)} %all-to-all-done.3.parts, bf16[4096,256]{1,0:T(8,128)(2,1)} %rest.1), custom_call_target="tpu_custom_call", output_to_operand_aliasing={{0}: (1, {})} | custom-call | flops 1000000 | bytes 1000000 | tf_op jit(solution)/shard_map/finish/pallas_call | solution.py:319
  (1 shorter events, 0.0 us)
Async XLA Ops:
  0.6 22.7 %copy-start.5 = (s32[3,256]{1,0:T(4,128)S(1)}, s32[3,256]{1,0:T(4,128)}, u32[]{:S(2)}) copy-start(s32[3,256]{1,0:T(4,128)} %miller.4) | copy-start | bytes 9220
  0.6 22.7 %copy-start.6 = (f32[16,256]{1,0:T(8,128)S(1)}, f32[16,256]{1,0:T(8,128)}, u32[]{:S(2)}) copy-start(f32[16,256]{1,0:T(8,128)} %filter_weight.1) | copy-start | bytes 49156
  8.0 4.6 %collective-permute-start = (bf16[256,512]{1,0:T(8,128)(2,1)}, bf16[256,512]{1,0:T(8,128)(2,1)S(1)}, u32[]{:S(2)}, u32[]{:S(2)}) collective-permute-start(bf16[256,512]{1,0:T(8,128)(2,1)} %get-tuple-element.23), channel_id=1, source_target_pairs={{0,8},{8,0},{1,9},{9,1},{2,10},{10,2},{3,11},{11,3},{4,12},{12,4},... | collective-permute-start | bytes 786440 | tf_op jit(solution)/shard_map/ppermute | solution.py:450
  12.6 0.9 copy-start.3
  14.3 19.5 %all-to-all-start = ((bf16[16,16,512]{2,1,0:T(8,128)(2,1)}), bf16[16,16,512]{2,1,0:T(8,128)(2,1)S(1)}, u32[]{:S(2)}, u32[]{:S(2)}) async-start(bf16[16,16,512]{2,1,0:T(8,128)(2,1)} %bitcast.2), calls=%async_computation | async-start | bytes 524288 | tf_op jit(solution)/shard_map/all_to_all | solution.py:433
  23.9 0.7 copy-start.7
  48.4 10.0 %copy-start.2 = (bf16[16,16,512]{2,1,0:T(8,128)(2,1)}, bf16[16,16,512]{2,1,0:T(8,128)(2,1)S(1)}, u32[]{:S(2)}) copy-start(bf16[16,16,512]{2,1,0:T(8,128)(2,1)S(1)} %all_to_all.20) | copy-start | bytes 786436
  49.6 18.5 %all-to-all-start.2 = ((bf16[8,272,256]{2,1,0:T(8,128)(2,1)}), bf16[8,272,256]{2,1,0:T(8,128)(2,1)S(1)}, u32[]{:S(2)}, u32[]{:S(2)}) async-start(bf16[8,272,256]{2,1,0:T(8,128)(2,1)} %copies.1), calls=%async_computation.2 | async-start | bytes 2228224 | tf_op jit(solution)/shard_map/all_to_all | solution.py:433
  53.8 4.6 %collective-permute-start.1 = (bf16[256,512]{1,0:T(8,128)(2,1)S(1)}, bf16[256,512]{1,0:T(8,128)(2,1)S(1)}, u32[]{:S(2)}, u32[]{:S(2)}) collective-permute-start(bf16[256,512]{1,0:T(8,128)(2,1)S(1)} %bitcast.6), channel_id=1, source_target_pairs={{0,8},{8,0},{1,9},{9,1},{2,10},{10,2},{3,11},{11,3},{4,12},{12,4},... | collective-permute-start | bytes 786440 | tf_op jit(solution)/shard_map/ppermute | solution.py:461
  58.4 0.7 copy-start.8
  68.1 4.6 %copy-start.4 = (bf16[48,256]{1,0:T(8,128)(2,1)S(1)}, bf16[48,256]{1,0:T(8,128)(2,1)}, u32[]{:S(2)}) copy-start(bf16[48,256]{1,0:T(8,128)(2,1)} %forces.1.force) | copy-start | bytes 73732
  68.1 3.8 %copy-start = (bf16[8,272,256]{2,1,0:T(8,128)(2,1)}, bf16[8,272,256]{2,1,0:T(8,128)(2,1)S(1)}, u32[]{:S(2)}) copy-start(bf16[8,272,256]{2,1,0:T(8,128)(2,1)S(1)} %all-to-all-done.2.mine) | copy-start | bytes 3342340
  68.1 4.5 %collective-permute-start.2 = (bf16[8,272,256]{2,1,0:T(8,128)(2,1)S(1)}, bf16[8,272,256]{2,1,0:T(8,128)(2,1)S(1)}, u32[]{:S(2)}, u32[]{:S(2)}) collective-permute-start(bf16[8,272,256]{2,1,0:T(8,128)(2,1)S(1)} %all-to-all-done.2.mine), channel_id=1, source_target_pairs={{0,8},{8,0},{1,9},{9,1},{2,10},{10,2},{3,11},{11,3},{4,12},{12,4},... | collective-permute-start | bytes 3342344 | tf_op jit(solution)/shard_map/ppermute | solution.py:465
  72.7 1.6 %copy-start.1 = (bf16[8,272,256]{2,1,0:T(8,128)(2,1)}, bf16[8,272,256]{2,1,0:T(8,128)(2,1)S(1)}, u32[]{:S(2)}) copy-start(bf16[8,272,256]{2,1,0:T(8,128)(2,1)S(1)} %collective-permute-done.2.other) | copy-start | bytes 3342340
  74.2 20.8 %all-to-all-start.3 = ((bf16[8,304,256]{2,1,0:T(8,128)(2,1)}), bf16[8,304,256]{2,1,0:T(8,128)(2,1)S(1)}, u32[]{:S(2)}, u32[]{:S(2)}) async-start(bf16[8,304,256]{2,1,0:T(8,128)(2,1)} %share.1), calls=%async_computation.3 | async-start | bytes 2490368 | tf_op jit(solution)/shard_map/all_to_all | solution.py:433
